TPU v7x, 256 devices: a whole 4x4x8 slice. The times are simulated.
256 devices in a mesh: pole: 8 (over z), row: 4 (over x_hi, core), col: 8 (over y, x_lo).
Axes of the slice: x: 4 (x_hi: 2, x_lo: 2; x = x_hi * 2 + x_lo), y: 4, z: 8, core: 2. Of those that a mesh axis runs over, the one named last changes fastest.
Arguments:
- ainv: float32 [8, 8192, 8192], P('pole', 'row', 'col'), may hold values from -6 to 6
- lfac: float32 [8, 8192, 384], P('pole', ('row', 'col')), may hold values from -0.0625 to 0.0625
- dinv: float32 [8, 384, 384], P('pole'), may hold values from -6 to 6
- weights: float32 [8], P('pole'), may hold values from 0.1 to 1
- present: int32 [32], replicated, may hold values 0 or 1
Outputs:
- ainv_col: float32 [8, 8192, 384], P('pole', ('row', 'col'))
- ainv_diag: float32 [8, 384, 384], P('pole')
- dm_col: float32 [8192, 384], P(('row', 'col'))
- dm_diag: float32 [384, 384], replicated
All inputs are finite; a program needn't handle non-finite values.
Results may differ from a plain program's by a relative error of at most 0.000071.
Values sent between devices are 32-bit elements; how exact they have to be, the bound alone decides.
No kernel may reach another device: no remote copies, remote signals or barrier semaphores. Data moves between devices by JAX's collectives and lax.ppermute only.
A program may use at most 128 MiB of HBM per device.

v0:
```python
import jax
import jax.numpy as jnp
from jax import lax
from jax.experimental import pallas as pl
from jax.experimental.pallas import tpu as pltpu
from jax.sharding import PartitionSpec as P

PLANE = ("row", "col")
MIB = 1 << 20


def place(x, y, core):
    return ((x // 2) * 2 + core) * 8 + y * 2 + x % 2


CHIPS = [(x, y, core) for x in range(4) for y in range(4) for core in range(2)]


def shift(value, dx=0, dy=0, other=0):
    pairs = [(place(x, y, c), place((x + dx) % 4, (y + dy) % 4, c ^ other)) for x, y, c in CHIPS]
    return lax.ppermute(value, PLANE, pairs)


def flip_x(value):
    return lax.ppermute(value, PLANE, [(place(x, y, c), place(x ^ 1, y, c)) for x, y, c in CHIPS])


def along_pole(value, step):
    return lax.ppermute(value, "pole", [(z, (z + step) % 8) for z in range(8)])


def pole_pair(value):
    return lax.ppermute(value, "pole", [(z, z ^ 1) for z in range(8)])


def panel_slot(value, j):
    pairs = []
    for x, y, c in CHIPS:
        k = 2 * c + (j ^ (x // 2))
        source = place((y // 2) * 2 + k % 2, 2 * (x % 2) + k // 2, y % 2)
        pairs.append((source, place(x, y, c)))
    return lax.ppermute(value, PLANE, pairs)


def split(value):
    high = value.astype(jnp.bfloat16)
    return high, (value - high.astype(jnp.float32)).astype(jnp.bfloat16)


def mm(a, b, contract=((1,), (0,))):
    return lax.dot_general(a, b, (contract, ((), ())), preferred_element_type=jnp.float32)


def mm3(a_high, a_low, b_high, b_low, contract=((1,), (0,))):
    return mm(a_high, b_high, contract) + (mm(a_high, b_low, contract) + mm(a_low, b_high, contract))


def split_kernel(value, high, low):
    rows = value.shape[0]

    def tile(t, _):
        at = pl.ds(pl.multiple_of(t * TILE, TILE), TILE)
        high[at, :], low[at, :] = split(value[at, :])
        return 0

    lax.fori_loop(0, rows // TILE, tile, 0)


TILE = 256
VMEM = pl.BlockSpec(memory_space=pltpu.VMEM)
SMEM = pl.BlockSpec(memory_space=pltpu.SMEM)


def local(kernel, in_specs, out_shape, flops, moved, scratch=()):
    return pl.pallas_call(
        kernel,
        out_shape=out_shape,
        in_specs=in_specs,
        out_specs=[VMEM] * len(out_shape),
        scratch_shapes=list(scratch),
        cost_estimate=pl.CostEstimate(flops=flops, bytes_accessed=moved, transcendentals=0),
        compiler_params=pltpu.CompilerParams(vmem_limit_bytes=16 * MIB),
    )


def split_inverse(inverse):
    rows, depth = inverse.shape
    out_shape = [jax.ShapeDtypeStruct((rows, depth), jnp.bfloat16)] * 2
    return local(split_kernel, [VMEM], out_shape, 4 * rows * depth, 8 * rows * depth)(inverse)


def block_dot(block, rows, a_high, a_low, high, low):
    at = pl.ds(pl.multiple_of(block * rows, rows), rows)
    return mm3(a_high[at, :], a_low[at, :], high[...], low[...])


def half_dot(block, side, rows, a_high, a_low, high, low):
    depth = high.shape[0]
    at = pl.ds(pl.multiple_of(block * rows, rows), rows)
    over = pl.ds(pl.multiple_of(side * depth, depth), depth)
    return mm3(a_high[at, over], a_low[at, over], high[...], low[...])


def own_kernel(info, s0, s1, a_high, a_low, up, down, high, low):
    rows = s0.shape[0]
    for i, slot in enumerate((s0, s1)):
        at = pl.ds(pl.multiple_of(info[3 + i] * rows, rows), rows)
        keep = (info[5 + i] > 0).astype(jnp.float32)
        high[at, :], low[at, :] = split(slot[...] * keep)
    up[...] = half_dot(info[0], info[2], rows, a_high, a_low, high, low)
    down[...] = half_dot(info[1], info[2], rows, a_high, a_low, high, low)


def rest_kernel(info, t0, t1, up_own, down_own, high_own, low_own, a_high, a_low, up, down, high, low, high_t, low_t):
    rows = t0.shape[0]
    for i, slot in enumerate((t0, t1)):
        at = pl.ds(pl.multiple_of(info[3 + i] * rows, rows), rows)
        keep = (info[5 + i] > 0).astype(jnp.float32)
        high_t[at, :], low_t[at, :] = split(slot[...] * keep)
    side = info[2]
    up[...] = up_own[...] + half_dot(info[0], side, rows, a_high, a_low, high_t, low_t)
    down[...] = down_own[...] + half_dot(info[1], side, rows, a_high, a_low, high_t, low_t)
    here = pl.ds(pl.multiple_of(side * 2 * rows, 2 * rows), 2 * rows)
    there = pl.ds(pl.multiple_of((1 - side) * 2 * rows, 2 * rows), 2 * rows)
    high[here, :], low[here, :] = high_t[...], low_t[...]
    high[there, :], low[there, :] = high_own[...], low_own[...]


def next_kernel(info, high, low, a_high, a_low, *outs):
    for i, out in enumerate(outs):
        out[...] = block_dot(info[i], out.shape[0], a_high, a_low, high, low)


def own_dot(info, halves, slots):
    rows, width = slots[0].shape
    out_shape = [jax.ShapeDtypeStruct((rows, width), jnp.float32)] * 2
    out_shape += [jax.ShapeDtypeStruct((2 * rows, width), jnp.bfloat16)] * 2
    return local(
        own_kernel, [SMEM] + [VMEM] * 4, out_shape, 24 * rows * rows * width, 8 * rows * (2 * rows + 3 * width)
    )(info, *slots, *halves)


def rest_dot(info, halves, slots, done):
    rows, width = slots[0].shape
    out_shape = [jax.ShapeDtypeStruct((rows, width), jnp.float32)] * 2
    out_shape += [jax.ShapeDtypeStruct((4 * rows, width), jnp.bfloat16)] * 2
    scratch = [pltpu.VMEM((2 * rows, width), jnp.bfloat16)] * 2
    return local(
        rest_kernel,
        [SMEM] + [VMEM] * 8,
        out_shape,
        24 * rows * rows * width,
        8 * rows * (2 * rows + 5 * width),
        scratch,
    )(info, *slots, *done, *halves)


def next_dot(info, halves, panel, rows, count):
    depth, width = panel[0].shape
    out_shape = [jax.ShapeDtypeStruct((rows, width), jnp.float32)] * count
    return local(
        next_kernel,
        [SMEM] + [VMEM] * 4,
        out_shape,
        count * 6 * rows * depth * width,
        count * 4 * rows * (depth + width),
    )(info, *panel, *halves)


def turn_kernel(own, other, own_high, own_low, other_high, other_low):
    own_high[...], own_low[...] = split(own[...].T)
    other_high[...], other_low[...] = split(other[...].T)


def turned(own, other):
    rows, width = own.shape
    out_shape = [jax.ShapeDtypeStruct((width, rows), jnp.bfloat16)] * 4
    return local(turn_kernel, [VMEM] * 2, out_shape, 8 * rows * width, 16 * rows * width)(own, other)


def corr_kernel(info, p0, p1, up0, down0, up1, down1, oh, ol, th, tl, corr, sum_own, sum_other):
    first = p0[...] + (up0[...] + down0[...])
    second = p1[...] + (up1[...] + down1[...])
    own_is_first = info[0] == 0
    mine = jnp.where(own_is_first, first, second) * (info[1] > 0).astype(jnp.float32)
    others = jnp.where(own_is_first, second, first) * (info[2] > 0).astype(jnp.float32)
    sum_own[...] = mine
    sum_other[...] = others
    corr[...] = mm3(oh[...], ol[...], *split(mine)) + mm3(th[...], tl[...], *split(others))


def correction(info, *arrays):
    rows, width = arrays[0].shape
    out_shape = [jax.ShapeDtypeStruct((n, width), jnp.float32) for n in (width, rows, rows)]
    return local(
        corr_kernel, [SMEM] + [VMEM] * len(arrays), out_shape, 12 * rows * width * width, 48 * rows * width
    )(info, *arrays)


def column_kernel(weight, mine, arrived, column, weighted):
    whole = mine[...] + arrived[...]
    column[...] = -whole
    eighth = whole.shape[0] // 8
    for i in range(8):
        at = (i % 4 * 2 + i // 4) * eighth
        weighted[i * eighth : (i + 1) * eighth, :] = -weight[0] * whole[at : at + eighth, :]


def inverse_column(weight, mine, arrived):
    rows, width = mine.shape
    out_shape = [jax.ShapeDtypeStruct((rows, width), jnp.float32)] * 2
    return local(column_kernel, [SMEM] + [VMEM] * 2, out_shape, 3 * rows * width, 16 * rows * width)(
        weight, mine, arrived
    )


def part(value, index, size):
    return lax.dynamic_slice_in_dim(value, index * size, size, 0)


def in_ring_order(value, arrived, me, axis=0):
    size = value.shape[axis]
    rising = [arrived[2], arrived[1], arrived[0], value]
    twice = jnp.concatenate(rising + rising[:3], axis)
    return lax.dynamic_slice_in_dim(twice, (3 - me) * size, 4 * size, axis)


def in_pair_order(value, other, me, axis=0):
    size = value.shape[axis]
    thrice = jnp.concatenate([other, value, other], axis)
    return lax.dynamic_slice_in_dim(thrice, (1 - me) * size, 2 * size, axis)


def on_device(ainv, lfac, dinv, weights, present):
    own = lfac[0]
    rows, width = own.shape
    row, col = lax.axis_index("row"), lax.axis_index("col")
    z = lax.axis_index("pole")
    x_hi, core = row // 2, row % 2
    y, x_lo = col // 2, col % 2
    half, quarter = width // 2, width // 8
    weight = weights[0]

    def sibling(v):
        return shift(v, other=1)

    slots = [panel_slot(own, 0), panel_slot(own, 1)]
    order = jnp.stack([2 * core + x_hi, 2 * core + 1 - x_hi, 2 * (1 - core) + x_hi, 2 * (1 - core) + 1 - x_hi])
    keep = jnp.take(present, jnp.concatenate([4 * col + order, row * 8 + jnp.stack([col, col ^ 1])]))

    def block(d, x_lo):
        return 2 * ((y + d) % 4) + x_lo

    far = jnp.stack([block(2, 0), block(2, 1)])
    places = jnp.stack([x_hi, 1 - x_hi])
    info = jnp.concatenate([far, core[None], places, keep[:2]]).astype(jnp.int32)
    rest = jnp.concatenate([far, 1 - core[None], places, keep[2:4]]).astype(jnp.int32)
    straight = jnp.stack([block(1, 1), block(3, 0)]).astype(jnp.int32)
    joined = jnp.stack([block(1, 0), block(3, 1)]).astype(jnp.int32)
    here = jnp.stack([block(0, 0), block(0, 1)]).astype(jnp.int32)
    tail = jnp.concatenate([x_lo[None], keep[4:]]).astype(jnp.int32)
    dinv_part = lax.dynamic_slice_in_dim(dinv[0], core * half + y * quarter, quarter, 0)
    halves = split_inverse(ainv[0])
    info, rest, straight, joined, here, tail, dinv_part, halves, slots = lax.optimization_barrier(
        (info, rest, straight, joined, here, tail, dinv_part, halves, slots)
    )
    others = [sibling(s) for s in slots]

    up, down, high, low = rest_dot(rest, halves, others, own_dot(info, halves, slots))
    panel = (high, low)
    up, down = shift(up, dy=1), shift(down, dy=-1)
    p11, p30 = next_dot(straight, halves, panel, rows, 2)
    up1, down0 = shift(p11, dy=1), shift(p30, dy=-1)
    p10, p31 = next_dot(joined, halves, panel, rows, 2)
    up0, down1 = shift(p10 + up, dy=1), shift(p31 + down, dy=-1)
    p00, p01 = next_dot(here, halves, panel, rows, 2)
    corr, sum_own, sum_other = correction(tail, p00, p01, up0, down0, up1, down1, *turned(own, flip_x(own)))

    pair, four = z % 2, z // 2
    eighth, middle = rows // 8, rows // 2
    column, weighted = inverse_column(weights, sum_own, flip_x(sum_other))
    dm = part(weighted, pair, middle) + pole_pair(part(weighted, 1 - pair, middle))

    steps = (1, 2, 3)
    mine = part(corr, core, half) + sibling(part(corr, 1 - core, half))
    away = [shift(part(mine, (y + k) % 4, quarter), dy=k) for k in steps]
    mine = (part(mine, y, quarter) + away[1]) + (away[0] + away[2])
    away = [shift(mine, dx=k) for k in steps]
    diagonal = dinv_part + ((mine + away[1]) + (away[0] + away[2]))
    paired = weight * diagonal
    paired = paired + pole_pair(paired)

    away = [along_pole(jnp.concatenate([part(dm, (four + k) % 4, eighth), paired]), 2 * k) for k in steps]
    summed = (jnp.concatenate([part(dm, four, eighth), paired]) + away[1]) + (away[0] + away[2])

    both = jnp.stack([diagonal, summed[eighth:]])
    both = in_ring_order(both, [shift(both, dy=k) for k in steps], y, 1)
    both = in_pair_order(both, sibling(both), core, 1)
    dm = summed[:eighth]
    dm = in_pair_order(dm, pole_pair(dm), pair)
    dm = in_ring_order(dm, [along_pole(dm, 2 * k) for k in steps], four)

    return column[None], both[:1], dm, both[1]


def solution(mesh):
    return jax.shard_map(
        on_device,
        mesh=mesh,
        in_specs=(
            P("pole", "row", "col"),
            P("pole", ("row", "col"), None),
            P("pole", None, None),
            P("pole"),
            P(),
        ),
        out_specs=(
            P("pole", ("row", "col"), None),
            P("pole", None, None),
            P(("row", "col"), None),
            P(),
        ),
        check_vma=False,
    )
```

profile of v0, /device:TPU:8, one launch (start us, length us, event | category | flops | bytes accessed | tf_op | source)
XLA Modules:
  0.0 125.4 jit_solution(2871835261453054208)
XLA Ops:
  0.6 2.1 %collective-permute-start = (f32[256,384]{1,0:T(8,128)}, f32[256,384]{1,0:T(8,128)S(1)}, u32[]{:S(2)}, u32[]{:S(2)}) collective-permute-start(f32[256,384]{1,0:T(8,128)} %bitcast.37), channel_id=1, source_target_pairs={{0,0},{2,8},{8,2},{10,10},{16,4},{18,12},{24,6},{26,14},{4,1},{6,9... | collective-permute-start | bytes 1179656 | tf_op jit(solution)/shard_map/ppermute | solution.py:42
  2.7 5.7 %collective-permute-start.1 = (f32[256,384]{1,0:T(8,128)}, f32[256,384]{1,0:T(8,128)S(1)}, u32[]{:S(2)}, u32[]{:S(2)}) collective-permute-start(f32[256,384]{1,0:T(8,128)} %bitcast.38), channel_id=1, source_target_pairs={{1,0},{3,8},{9,2},{11,10},{17,4},{19,12},{25,6},{27,14},{5,1},{7,9... | collective-permute-start | bytes 1179656 | tf_op jit(solution)/shard_map/ppermute | solution.py:42
  8.8 1.3 %gather_fusion = s32[6]{0:T(128)S(1)} fusion(s32[32]{0:T(128)} %param.9, s32[1024]{0:T(1024)S(1)} %pad_clamp_fusion), kind=kCustom, calls=%fused_computation | custom fusion | bytes 72 | tf_op jit(solution)/shard_map/jit(_take)/gather | solution.py:249
  10.5 3.4 %copy-done.5 = f32[1,2048,1024]{2,1,0:T(8,128)S(1)} copy-done((f32[1,2048,1024]{2,1,0:T(8,128)S(1)}, f32[1,2048,1024]{2,1,0:T(8,128)}, u32[]{:S(2)}) %copy-start.5) | copy-done | bytes 8388632
  13.9 1.1 shard_map.84
  15.2 3.6 %collective-permute-done.s0 = f32[256,384]{1,0:T(8,128)S(1)} collective-permute-done((f32[256,384]{1,0:T(8,128)}, f32[256,384]{1,0:T(8,128)S(1)}, u32[]{:S(2)}, u32[]{:S(2)}) %collective-permute-start) | collective-permute-done | bytes 393248 | tf_op jit(solution)/shard_map/ppermute | solution.py:42
  19.3 1.7 %shard_map.85 = (f32[256,384]{1,0:T(8,128)S(1)}, f32[256,384]{1,0:T(8,128)S(1)}, bf16[512,384]{1,0:T(8,128)(2,1)S(1)}, bf16[512,384]{1,0:T(8,128)(2,1)S(1)}) custom-call(s32[7]{0:T(128)S(1)} %concatenate.93.info, f32[256,384]{1,0:T(8,128)S(1)} %collective-permute-done.s0, f32[256,384]{1,0:T(8,128)S(1)} %collective-permute-done.1.s1, ...), custom_call_target="tpu_custom_call" | custom-call | flops 603979776 | bytes 3407872 | tf_op jit(solution)/shard_map/pallas_call | solution.py:138
  21.1 1.9 %shard_map.86 = (f32[256,384]{1,0:T(8,128)S(1)}, f32[256,384]{1,0:T(8,128)S(1)}, bf16[1024,384]{1,0:T(8,128)(2,1)S(1)}, bf16[1024,384]{1,0:T(8,128)(2,1)S(1)}) custom-call(s32[7]{0:T(128)S(1)} %concatenate.94.info, f32[256,384]{1,0:T(8,128)S(1)} %collective-permute-done.2.t0, f32[256,384]{1,0:T(8,128)S(1)} %collective-permute-done.3.t1, ...), custom_call_target="tpu_custom_call" | custom-call | flops 603979776 | bytes 4980736 | tf_op jit(solution)/shard_map/pallas_call | solution.py:148
  23.6 8.8 %collective-permute-start.4 = (f32[256,384]{1,0:T(8,128)S(1)}, f32[256,384]{1,0:T(8,128)S(1)}, u32[]{:S(2)}, u32[]{:S(2)}) collective-permute-start(f32[256,384]{1,0:T(8,128)S(1)} %get-tuple-element.60), channel_id=1, source_target_pairs={{0,2},{8,10},{2,4},{10,12},{4,6},{12,14},{6,0},{14,8},{1,3},{9,11}... | collective-permute-start | bytes 1179656 | tf_op jit(solution)/shard_map/ppermute | solution.py:21
  32.4 3.1 %shard_map.89 = (f32[256,384]{1,0:T(8,128)}, f32[256,384]{1,0:T(8,128)}) custom-call(s32[2]{0:T(128)S(1)} %get-tuple-element.61.info, bf16[1024,384]{1,0:T(8,128)(2,1)S(1)} %get-tuple-element.54.high, bf16[1024,384]{1,0:T(8,128)(2,1)S(1)} %get-tuple-element.55.low, bf16[2048,1024]{1,0:T(8,128)(2,1)S(1)} %get-tuple-element.48.a_high, ...), custom_call_target="tpu_custom_call" | custom-call | flops 1207959552 | bytes 2883584 | tf_op jit(solution)/shard_map/pallas_call | solution.py:161
  35.5 1.6 %collective-permute-start.6 = (f32[256,384]{1,0:T(8,128)}, f32[256,384]{1,0:T(8,128)S(1)}, u32[]{:S(2)}, u32[]{:S(2)}) collective-permute-start(f32[256,384]{1,0:T(8,128)} %get-tuple-element.62), channel_id=1, source_target_pairs={{0,6},{8,14},{2,0},{10,8},{4,2},{12,10},{6,4},{14,12},{1,7},{9,15}... | collective-permute-start | bytes 1179656 | tf_op jit(solution)/shard_map/ppermute | solution.py:21
  37.5 2.3 %shard_map.88 = (f32[256,384]{1,0:T(8,128)S(1)}, f32[256,384]{1,0:T(8,128)S(1)}) custom-call(s32[2]{0:T(128)S(1)} %get-tuple-element.58.info, bf16[1024,384]{1,0:T(8,128)(2,1)S(1)} %get-tuple-element.54.high, bf16[1024,384]{1,0:T(8,128)(2,1)S(1)} %get-tuple-element.55.low, bf16[2048,1024]{1,0:T(8,128)(2,1)S(1)} %get-tuple-element.48.a_high, ...), custom_call_target="tpu_custom_call" | custom-call | flops 1207959552 | bytes 2883584 | tf_op jit(solution)/shard_map/pallas_call | solution.py:161
  39.9 2.4 %collective-permute-done.8 = f32[256,384]{1,0:T(8,128)S(1)} collective-permute-done((f32[256,384]{1,0:T(8,128)S(1)}, f32[256,384]{1,0:T(8,128)S(1)}, u32[]{:S(2)}, u32[]{:S(2)}) %collective-permute-start.8) | collective-permute-done | bytes 393248 | tf_op jit(solution)/shard_map/ppermute | solution.py:21
  42.2 0.8 add.265
  43.0 1.3 %collective-permute-start.9 = (f32[256,384]{1,0:T(8,128)}, f32[256,384]{1,0:T(8,128)}, u32[]{:S(2)}, u32[]{:S(2)}) collective-permute-start(f32[256,384]{1,0:T(8,128)} %add.265), channel_id=1, source_target_pairs={{0,6},{8,14},{2,0},{10,8},{4,2},{12,10},{6,4},{14,12},{1,7},{9,15}... | collective-permute-start | bytes 1179656 | tf_op jit(solution)/shard_map/ppermute | solution.py:21
  44.3 0.8 add.264
  46.2 2.2 %copy-done.2 = bf16[2048,1024]{1,0:T(8,128)(2,1)S(1)} copy-done((bf16[2048,1024]{1,0:T(8,128)(2,1)S(1)}, bf16[2048,1024]{1,0:T(8,128)(2,1)}, u32[]{:S(2)}) %copy-start.2) | copy-done | bytes 4194328
  48.4 2.2 %copy-done.4 = bf16[2048,1024]{1,0:T(8,128)(2,1)S(1)} copy-done((bf16[2048,1024]{1,0:T(8,128)(2,1)S(1)}, bf16[2048,1024]{1,0:T(8,128)(2,1)}, u32[]{:S(2)}) %copy-start.4) | copy-done | bytes 4194328
  50.5 2.3 %shard_map.87 = (f32[256,384]{1,0:T(8,128)S(1)}, f32[256,384]{1,0:T(8,128)S(1)}) custom-call(s32[2]{0:T(128)S(1)} %pad_add_fusion.2.info, bf16[1024,384]{1,0:T(8,128)(2,1)S(1)} %get-tuple-element.54.high, bf16[1024,384]{1,0:T(8,128)(2,1)S(1)} %get-tuple-element.55.low, bf16[2048,1024]{1,0:T(8,128)(2,1)S(1)} %copy-done.2, bf16[2048,1024]{1,0:T(8,128)(2,1)S(1)} %copy-done.4), custom_call_target="tpu_custom_call" | custom-call | flops 1207959552 | bytes 2883584 | tf_op jit(solution)/shard_map/pallas_call | solution.py:161
  52.9 5.8 %collective-permute-done.9.down1 = f32[256,384]{1,0:T(8,128)} collective-permute-done((f32[256,384]{1,0:T(8,128)}, f32[256,384]{1,0:T(8,128)}, u32[]{:S(2)}, u32[]{:S(2)}) %collective-permute-start.9) | collective-permute-done | bytes 393248 | tf_op jit(solution)/shard_map/ppermute | solution.py:21
  58.7 1.4 %collective-permute-done.5.up0 = f32[256,384]{1,0:T(8,128)} collective-permute-done((f32[256,384]{1,0:T(8,128)}, f32[256,384]{1,0:T(8,128)}, u32[]{:S(2)}, u32[]{:S(2)}) %collective-permute-start.5) | collective-permute-done | bytes 393248 | tf_op jit(solution)/shard_map/ppermute | solution.py:21
  60.1 2.1 %shard_map.91 = (f32[384,384]{1,0:T(8,128)S(1)}, f32[256,384]{1,0:T(8,128)S(1)}, f32[256,384]{1,0:T(8,128)S(1)}) custom-call(s32[3]{0:T(128)S(1)} %pad_add_fusion.3.info, f32[256,384]{1,0:T(8,128)S(1)} %get-tuple-element.56.p0, f32[256,384]{1,0:T(8,128)S(1)} %get-tuple-element.57.p1, f32[256,384]{1,0:T(8,128)} %collective-permute-done.5.up0, ...), custom_call_target="tpu_custom_call" | custom-call | flops 452984832 | bytes 4718592 | tf_op jit(solution)/shard_map/pallas_call | solution.py:195
  62.5 1.4 %collective-permute-done.12 = f32[192,384]{1,0:T(8,128)S(1)} collective-permute-done((f32[192,384]{1,0:T(8,128)S(1)}, f32[192,384]{1,0:T(8,128)S(1)}, u32[]{:S(2)}, u32[]{:S(2)}) %collective-permute-start.12) | collective-permute-done | bytes 294944 | tf_op jit(solution)/shard_map/ppermute | solution.py:21
  64.0 2.2 %collective-permute-start.13 = (f32[48,384]{1,0:T(8,128)S(1)}, f32[48,384]{1,0:T(8,128)S(1)}, u32[]{:S(2)}, u32[]{:S(2)}) collective-permute-start(f32[48,384]{1,0:T(8,128)S(1)} %get-tuple-element.80), channel_id=1, source_target_pairs={{0,4},{8,12},{2,6},{10,14},{4,0},{12,8},{6,2},{14,10},{1,5},{9,13}... | collective-permute-start | bytes 221192 | tf_op jit(solution)/shard_map/ppermute | solution.py:21
  66.2 2.3 %collective-permute-start.14 = (f32[48,384]{1,0:T(8,128)S(1)}, f32[48,384]{1,0:T(8,128)S(1)}, u32[]{:S(2)}, u32[]{:S(2)}) collective-permute-start(f32[48,384]{1,0:T(8,128)S(1)} %get-tuple-element.82), channel_id=1, source_target_pairs={{0,2},{8,10},{2,4},{10,12},{4,6},{12,14},{6,0},{14,8},{1,3},{9,11}... | collective-permute-start | bytes 221192 | tf_op jit(solution)/shard_map/ppermute | solution.py:21
  69.9 1.2 collective-permute-done.14
  71.2 1.7 %collective-permute-done.15 = f32[48,384]{1,0:T(8,128)S(1)} collective-permute-done((f32[48,384]{1,0:T(8,128)S(1)}, f32[48,384]{1,0:T(8,128)S(1)}, u32[]{:S(2)}, u32[]{:S(2)}) %collective-permute-start.15) | collective-permute-done | bytes 73760 | tf_op jit(solution)/shard_map/ppermute | solution.py:21
  72.9 0.9 collective-permute-start.16
  73.7 0.8 collective-permute-start.17
  74.6 2.4 %collective-permute-start.18 = (f32[48,384]{1,0:T(8,128)S(1)}, f32[48,384]{1,0:T(8,128)S(1)}, u32[]{:S(2)}, u32[]{:S(2)}) collective-permute-start(f32[48,384]{1,0:T(8,128)S(1)} %add_add_fusion.1), channel_id=1, source_target_pairs={{0,17},{8,25},{2,19},{10,27},{4,21},{12,29},{6,23},{14,31},{1,0},{... | collective-permute-start | bytes 221192 | tf_op jit(solution)/shard_map/ppermute | solution.py:21
  77.8 2.0 %collective-permute-start.19 = (f32[128,384]{1,0:T(8,128)S(1)}, f32[128,384]{1,0:T(8,128)S(1)}, u32[]{:S(2)}, u32[]{:S(2)}) collective-permute-start(f32[128,384]{1,0:T(8,128)S(1)} %constant_dynamic-slice_fusion.6), channel_id=1, source_target_pairs={{0,32},{32,0},{64,96},{96,64},{128,160},{160,128},{192,224},{224,1... | collective-permute-start | bytes 589832 | tf_op jit(solution)/shard_map/ppermute | solution.py:33
  79.8 2.0 %collective-permute-start.20 = (f32[48,384]{1,0:T(8,128)S(1)}, f32[48,384]{1,0:T(8,128)S(1)}, u32[]{:S(2)}, u32[]{:S(2)}) collective-permute-start(f32[48,384]{1,0:T(8,128)S(1)} %get-tuple-element.76), channel_id=1, source_target_pairs={{0,32},{32,0},{64,96},{96,64},{128,160},{160,128},{192,224},{224,1... | collective-permute-start | bytes 221192 | tf_op jit(solution)/shard_map/ppermute | solution.py:33
  81.9 3.0 %collective-permute-done.20 = f32[48,384]{1,0:T(8,128)S(1)} collective-permute-done((f32[48,384]{1,0:T(8,128)S(1)}, f32[48,384]{1,0:T(8,128)S(1)}, u32[]{:S(2)}, u32[]{:S(2)}) %collective-permute-start.20) | collective-permute-done | bytes 73760 | tf_op jit(solution)/shard_map/ppermute | solution.py:33
  85.1 7.4 %collective-permute-start.21 = (f32[80,384]{1,0:T(8,128)S(1)}, f32[80,384]{1,0:T(8,128)S(1)}, u32[]{:S(2)}, u32[]{:S(2)}) collective-permute-start(f32[80,384]{1,0:T(8,128)S(1)} %get-tuple-element.88), channel_id=1, source_target_pairs={{0,128},{32,160},{64,192},{96,224},{128,0},{160,32},{192,64},{224,... | collective-permute-start | bytes 368648 | tf_op jit(solution)/shard_map/ppermute | solution.py:29
  92.4 1.2 collective-permute-start.22
  93.6 2.9 %collective-permute-start.23 = (f32[80,384]{1,0:T(8,128)S(1)}, f32[80,384]{1,0:T(8,128)S(1)}, u32[]{:S(2)}, u32[]{:S(2)}) collective-permute-start(f32[80,384]{1,0:T(8,128)S(1)} %get-tuple-element.87), channel_id=1, source_target_pairs={{0,192},{32,224},{64,0},{96,32},{128,64},{160,96},{192,128},{224,1... | collective-permute-start | bytes 368648 | tf_op jit(solution)/shard_map/ppermute | solution.py:29
  97.0 3.9 %collective-permute-done.22 = f32[80,384]{1,0:T(8,128)S(1)} collective-permute-done((f32[80,384]{1,0:T(8,128)S(1)}, f32[80,384]{1,0:T(8,128)S(1)}, u32[]{:S(2)}, u32[]{:S(2)}) %collective-permute-start.22) | collective-permute-done | bytes 122912 | tf_op jit(solution)/shard_map/ppermute | solution.py:29
  100.9 1.2 collective-permute-done.23
  102.1 0.9 collective-permute-start.28
  103.1 2.3 %collective-permute-start.24 = (f32[2,48,384]{2,1,0:T(8,128)S(1)}, f32[2,48,384]{2,1,0:T(8,128)S(1)}, u32[]{:S(2)}, u32[]{:S(2)}) collective-permute-start(f32[2,48,384]{2,1,0:T(8,128)S(1)} %pad_maximum_fusion.4), channel_id=1, source_target_pairs={{0,6},{8,14},{2,0},{10,8},{4,2},{12,10},{6,4},{14,12},{1,7},{9,15}... | collective-permute-start | bytes 442376 | tf_op jit(solution)/shard_map/ppermute | solution.py:21
  105.3 1.7 %collective-permute-start.25 = (f32[2,48,384]{2,1,0:T(8,128)S(1)}, f32[2,48,384]{2,1,0:T(8,128)S(1)}, u32[]{:S(2)}, u32[]{:S(2)}) collective-permute-start(f32[2,48,384]{2,1,0:T(8,128)S(1)} %pad_maximum_fusion.4), channel_id=1, source_target_pairs={{0,4},{8,12},{2,6},{10,14},{4,0},{12,8},{6,2},{14,10},{1,5},{9,13}... | collective-permute-start | bytes 442376 | tf_op jit(solution)/shard_map/ppermute | solution.py:21
  107.0 2.5 %collective-permute-start.26 = (f32[2,48,384]{2,1,0:T(8,128)S(1)}, f32[2,48,384]{2,1,0:T(8,128)S(1)}, u32[]{:S(2)}, u32[]{:S(2)}) collective-permute-start(f32[2,48,384]{2,1,0:T(8,128)S(1)} %pad_maximum_fusion.4), channel_id=1, source_target_pairs={{0,2},{8,10},{2,4},{10,12},{4,6},{12,14},{6,0},{14,8},{1,3},{9,11}... | collective-permute-start | bytes 442376 | tf_op jit(solution)/shard_map/ppermute | solution.py:21
  109.5 3.0 %collective-permute-start.29 = (f32[64,384]{1,0:T(8,128)S(1)}, f32[64,384]{1,0:T(8,128)S(1)}, u32[]{:S(2)}, u32[]{:S(2)}) collective-permute-start(f32[64,384]{1,0:T(8,128)S(1)} %fusion.5), channel_id=1, source_target_pairs={{0,192},{32,224},{64,0},{96,32},{128,64},{160,96},{192,128},{224,1... | collective-permute-start | bytes 294920 | tf_op jit(solution)/shard_map/ppermute | solution.py:29
  112.6 1.3 %collective-permute-start.30 = (f32[64,384]{1,0:T(8,128)S(1)}, f32[64,384]{1,0:T(8,128)S(1)}, u32[]{:S(2)}, u32[]{:S(2)}) collective-permute-start(f32[64,384]{1,0:T(8,128)S(1)} %fusion.5), channel_id=1, source_target_pairs={{0,128},{32,160},{64,192},{96,224},{128,0},{160,32},{192,64},{224,... | collective-permute-start | bytes 294920 | tf_op jit(solution)/shard_map/ppermute | solution.py:29
  113.9 1.1 collective-permute-start.31
  115.3 1.2 collective-permute-done.29
  116.5 6.0 %collective-permute-done.30 = f32[64,384]{1,0:T(8,128)S(1)} collective-permute-done((f32[64,384]{1,0:T(8,128)S(1)}, f32[64,384]{1,0:T(8,128)S(1)}, u32[]{:S(2)}, u32[]{:S(2)}) %collective-permute-start.30) | collective-permute-done | bytes 98336 | tf_op jit(solution)/shard_map/ppermute | solution.py:29
  124.3 1.1 slice_bitcast_fusion
  (89 shorter events, 8.2 us)
Async XLA Ops:
  0.6 14.6 %copy-start = (f32[1,384,384]{2,1,0:T(8,128)S(1)}, f32[1,384,384]{2,1,0:T(8,128)}, u32[]{:S(2)}) copy-start(f32[1,384,384]{2,1,0:T(8,128)} %param.7) | copy-start | bytes 1769476
  0.6 18.1 %collective-permute-start = (f32[256,384]{1,0:T(8,128)}, f32[256,384]{1,0:T(8,128)S(1)}, u32[]{:S(2)}, u32[]{:S(2)}) collective-permute-start(f32[256,384]{1,0:T(8,128)} %bitcast.37), channel_id=1, source_target_pairs={{0,0},{2,8},{8,2},{10,10},{16,4},{18,12},{24,6},{26,14},{4,1},{6,9... | collective-permute-start | bytes 1179656 | tf_op jit(solution)/shard_map/ppermute | solution.py:42
  2.7 16.1 %collective-permute-start.1 = (f32[256,384]{1,0:T(8,128)}, f32[256,384]{1,0:T(8,128)S(1)}, u32[]{:S(2)}, u32[]{:S(2)}) collective-permute-start(f32[256,384]{1,0:T(8,128)} %bitcast.38), channel_id=1, source_target_pairs={{1,0},{3,8},{9,2},{11,10},{17,4},{19,12},{25,6},{27,14},{5,1},{7,9... | collective-permute-start | bytes 1179656 | tf_op jit(solution)/shard_map/ppermute | solution.py:42
  10.5 3.4 %copy-start.5 = (f32[1,2048,1024]{2,1,0:T(8,128)S(1)}, f32[1,2048,1024]{2,1,0:T(8,128)}, u32[]{:S(2)}) copy-start(f32[1,2048,1024]{2,1,0:T(8,128)} %param.5) | copy-start | bytes 25165828
  15.0 22.5 %copy-start.1 = (bf16[2048,1024]{1,0:T(8,128)(2,1)}, bf16[2048,1024]{1,0:T(8,128)(2,1)S(1)}, u32[]{:S(2)}) copy-start(bf16[2048,1024]{1,0:T(8,128)(2,1)S(1)} %get-tuple-element.48.a_high) | copy-start | bytes 12582916
  15.0 22.5 %copy-start.3 = (bf16[2048,1024]{1,0:T(8,128)(2,1)}, bf16[2048,1024]{1,0:T(8,128)(2,1)S(1)}, u32[]{:S(2)}) copy-start(bf16[2048,1024]{1,0:T(8,128)(2,1)S(1)} %get-tuple-element.49.a_low) | copy-start | bytes 12582916
  18.8 2.2 %collective-permute-start.2 = (f32[256,384]{1,0:T(8,128)S(1)}, f32[256,384]{1,0:T(8,128)S(1)}, u32[]{:S(2)}, u32[]{:S(2)}) collective-permute-start(f32[256,384]{1,0:T(8,128)S(1)} %collective-permute-done.s0), channel_id=1, source_target_pairs={{0,8},{8,0},{2,10},{10,2},{4,12},{12,4},{6,14},{14,6},{1,9},{9,1},... | collective-permute-start | bytes 1179656 | tf_op jit(solution)/shard_map/ppermute | solution.py:21
  18.8 2.3 %collective-permute-start.3 = (f32[256,384]{1,0:T(8,128)S(1)}, f32[256,384]{1,0:T(8,128)S(1)}, u32[]{:S(2)}, u32[]{:S(2)}) collective-permute-start(f32[256,384]{1,0:T(8,128)S(1)} %collective-permute-done.1.s1), channel_id=1, source_target_pairs={{0,8},{8,0},{2,10},{10,2},{4,12},{12,4},{6,14},{14,6},{1,9},{9,1},... | collective-permute-start | bytes 1179656 | tf_op jit(solution)/shard_map/ppermute | solution.py:21
  21.1 11.3 %copy-start.6 = (f32[1,256,384]{2,1,0:T(8,128)S(1)}, f32[1,256,384]{2,1,0:T(8,128)}, u32[]{:S(2)}) copy-start(f32[1,256,384]{2,1,0:T(8,128)} %param.6) | copy-start | bytes 1179652
  23.0 19.2 %collective-permute-start.8 = (f32[256,384]{1,0:T(8,128)S(1)}, f32[256,384]{1,0:T(8,128)S(1)}, u32[]{:S(2)}, u32[]{:S(2)}) collective-permute-start(f32[256,384]{1,0:T(8,128)S(1)} %get-tuple-element.65), channel_id=1, source_target_pairs={{0,6},{8,14},{2,0},{10,8},{4,2},{12,10},{6,4},{14,12},{1,7},{9,15}... | collective-permute-start | bytes 1179656 | tf_op jit(solution)/shard_map/ppermute | solution.py:21
  23.6 20.7 %collective-permute-start.4 = (f32[256,384]{1,0:T(8,128)S(1)}, f32[256,384]{1,0:T(8,128)S(1)}, u32[]{:S(2)}, u32[]{:S(2)}) collective-permute-start(f32[256,384]{1,0:T(8,128)S(1)} %get-tuple-element.60), channel_id=1, source_target_pairs={{0,2},{8,10},{2,4},{10,12},{4,6},{12,14},{6,0},{14,8},{1,3},{9,11}... | collective-permute-start | bytes 1179656 | tf_op jit(solution)/shard_map/ppermute | solution.py:21
  32.4 13.5 %collective-permute-start.10 = (f32[256,384]{1,0:T(8,128)S(1)}, f32[256,384]{1,0:T(8,128)S(1)}, u32[]{:S(2)}, u32[]{:S(2)}) collective-permute-start(f32[256,384]{1,0:T(8,128)S(1)} %bitcast.39), channel_id=1, source_target_pairs={{0,1},{8,9},{2,3},{10,11},{4,5},{12,13},{6,7},{14,15},{1,0},{9,8},... | collective-permute-start | bytes 1179656 | tf_op jit(solution)/shard_map/ppermute | solution.py:25
  35.5 17.4 %collective-permute-start.6 = (f32[256,384]{1,0:T(8,128)}, f32[256,384]{1,0:T(8,128)S(1)}, u32[]{:S(2)}, u32[]{:S(2)}) collective-permute-start(f32[256,384]{1,0:T(8,128)} %get-tuple-element.62), channel_id=1, source_target_pairs={{0,6},{8,14},{2,0},{10,8},{4,2},{12,10},{6,4},{14,12},{1,7},{9,15}... | collective-permute-start | bytes 1179656 | tf_op jit(solution)/shard_map/ppermute | solution.py:21
  37.1 15.8 %collective-permute-start.7 = (f32[256,384]{1,0:T(8,128)}, f32[256,384]{1,0:T(8,128)}, u32[]{:S(2)}, u32[]{:S(2)}) collective-permute-start(f32[256,384]{1,0:T(8,128)} %get-tuple-element.63), channel_id=1, source_target_pairs={{0,2},{8,10},{2,4},{10,12},{4,6},{12,14},{6,0},{14,8},{1,3},{9,11}... | collective-permute-start | bytes 1179656 | tf_op jit(solution)/shard_map/ppermute | solution.py:21
  43.0 15.7 %collective-permute-start.9 = (f32[256,384]{1,0:T(8,128)}, f32[256,384]{1,0:T(8,128)}, u32[]{:S(2)}, u32[]{:S(2)}) collective-permute-start(f32[256,384]{1,0:T(8,128)} %add.265), channel_id=1, source_target_pairs={{0,6},{8,14},{2,0},{10,8},{4,2},{12,10},{6,4},{14,12},{1,7},{9,15}... | collective-permute-start | bytes 1179656 | tf_op jit(solution)/shard_map/ppermute | solution.py:21
  45.1 15.0 %collective-permute-start.5 = (f32[256,384]{1,0:T(8,128)}, f32[256,384]{1,0:T(8,128)}, u32[]{:S(2)}, u32[]{:S(2)}) collective-permute-start(f32[256,384]{1,0:T(8,128)} %add.264), channel_id=1, source_target_pairs={{0,2},{8,10},{2,4},{10,12},{4,6},{12,14},{6,0},{14,8},{1,3},{9,11}... | collective-permute-start | bytes 1179656 | tf_op jit(solution)/shard_map/ppermute | solution.py:21
  46.2 2.2 %copy-start.2 = (bf16[2048,1024]{1,0:T(8,128)(2,1)S(1)}, bf16[2048,1024]{1,0:T(8,128)(2,1)}, u32[]{:S(2)}) copy-start(bf16[2048,1024]{1,0:T(8,128)(2,1)} %copy-done.1) | copy-start | bytes 12582916
  48.4 2.2 %copy-start.4 = (bf16[2048,1024]{1,0:T(8,128)(2,1)S(1)}, bf16[2048,1024]{1,0:T(8,128)(2,1)}, u32[]{:S(2)}) copy-start(bf16[2048,1024]{1,0:T(8,128)(2,1)} %copy-done.3) | copy-start | bytes 12582916
  62.3 1.7 %collective-permute-start.12 = (f32[192,384]{1,0:T(8,128)S(1)}, f32[192,384]{1,0:T(8,128)S(1)}, u32[]{:S(2)}, u32[]{:S(2)}) collective-permute-start(f32[192,384]{1,0:T(8,128)S(1)} %constant_dynamic-slice_fusion.10), channel_id=1, source_target_pairs={{0,8},{8,0},{2,10},{10,2},{4,12},{12,4},{6,14},{14,6},{1,9},{9,1},... | collective-permute-start | bytes 884744 | tf_op jit(solution)/shard_map/ppermute | solution.py:21
  62.4 14.6 %collective-permute-start.11 = (f32[256,384]{1,0:T(8,128)S(1)}, f32[256,384]{1,0:T(8,128)S(1)}, u32[]{:S(2)}, u32[]{:S(2)}) collective-permute-start(f32[256,384]{1,0:T(8,128)S(1)} %get-tuple-element.71), channel_id=1, source_target_pairs={{0,1},{8,9},{2,3},{10,11},{4,5},{12,13},{6,7},{14,15},{1,0},{9,8},... | collective-permute-start | bytes 1179656 | tf_op jit(solution)/shard_map/ppermute | solution.py:25
  64.0 5.9 %collective-permute-start.13 = (f32[48,384]{1,0:T(8,128)S(1)}, f32[48,384]{1,0:T(8,128)S(1)}, u32[]{:S(2)}, u32[]{:S(2)}) collective-permute-start(f32[48,384]{1,0:T(8,128)S(1)} %get-tuple-element.80), channel_id=1, source_target_pairs={{0,4},{8,12},{2,6},{10,14},{4,0},{12,8},{6,2},{14,10},{1,5},{9,13}... | collective-permute-start | bytes 221192 | tf_op jit(solution)/shard_map/ppermute | solution.py:21
  66.2 5.0 %collective-permute-start.14 = (f32[48,384]{1,0:T(8,128)S(1)}, f32[48,384]{1,0:T(8,128)S(1)}, u32[]{:S(2)}, u32[]{:S(2)}) collective-permute-start(f32[48,384]{1,0:T(8,128)S(1)} %get-tuple-element.82), channel_id=1, source_target_pairs={{0,2},{8,10},{2,4},{10,12},{4,6},{12,14},{6,0},{14,8},{1,3},{9,11}... | collective-permute-start | bytes 221192 | tf_op jit(solution)/shard_map/ppermute | solution.py:21
  68.5 4.4 %collective-permute-start.15 = (f32[48,384]{1,0:T(8,128)S(1)}, f32[48,384]{1,0:T(8,128)S(1)}, u32[]{:S(2)}, u32[]{:S(2)}) collective-permute-start(f32[48,384]{1,0:T(8,128)S(1)} %get-tuple-element.81), channel_id=1, source_target_pairs={{0,6},{8,14},{2,0},{10,8},{4,2},{12,10},{6,4},{14,12},{1,7},{9,15}... | collective-permute-start | bytes 221192 | tf_op jit(solution)/shard_map/ppermute | solution.py:21
  72.9 6.9 %collective-permute-start.16 = (f32[48,384]{1,0:T(8,128)S(1)}, f32[48,384]{1,0:T(8,128)S(1)}, u32[]{:S(2)}, u32[]{:S(2)}) collective-permute-start(f32[48,384]{1,0:T(8,128)S(1)} %add_add_fusion.1), channel_id=1, source_target_pairs={{0,16},{8,24},{2,18},{10,26},{4,20},{12,28},{6,22},{14,30},{1,17},... | collective-permute-start | bytes 221192 | tf_op jit(solution)/shard_map/ppermute | solution.py:21
  73.7 6.1 %collective-permute-start.17 = (f32[48,384]{1,0:T(8,128)S(1)}, f32[48,384]{1,0:T(8,128)S(1)}, u32[]{:S(2)}, u32[]{:S(2)}) collective-permute-start(f32[48,384]{1,0:T(8,128)S(1)} %add_add_fusion.1), channel_id=1, source_target_pairs={{0,1},{8,9},{2,3},{10,11},{4,5},{12,13},{6,7},{14,15},{1,16},{9,24... | collective-permute-start | bytes 221192 | tf_op jit(solution)/shard_map/ppermute | solution.py:21
  74.6 5.2 %collective-permute-start.18 = (f32[48,384]{1,0:T(8,128)S(1)}, f32[48,384]{1,0:T(8,128)S(1)}, u32[]{:S(2)}, u32[]{:S(2)}) collective-permute-start(f32[48,384]{1,0:T(8,128)S(1)} %add_add_fusion.1), channel_id=1, source_target_pairs={{0,17},{8,25},{2,19},{10,27},{4,21},{12,29},{6,23},{14,31},{1,0},{... | collective-permute-start | bytes 221192 | tf_op jit(solution)/shard_map/ppermute | solution.py:21
  77.8 7.2 %collective-permute-start.19 = (f32[128,384]{1,0:T(8,128)S(1)}, f32[128,384]{1,0:T(8,128)S(1)}, u32[]{:S(2)}, u32[]{:S(2)}) collective-permute-start(f32[128,384]{1,0:T(8,128)S(1)} %constant_dynamic-slice_fusion.6), channel_id=1, source_target_pairs={{0,32},{32,0},{64,96},{96,64},{128,160},{160,128},{192,224},{224,1... | collective-permute-start | bytes 589832 | tf_op jit(solution)/shard_map/ppermute | solution.py:33
  79.8 5.1 %collective-permute-start.20 = (f32[48,384]{1,0:T(8,128)S(1)}, f32[48,384]{1,0:T(8,128)S(1)}, u32[]{:S(2)}, u32[]{:S(2)}) collective-permute-start(f32[48,384]{1,0:T(8,128)S(1)} %get-tuple-element.76), channel_id=1, source_target_pairs={{0,32},{32,0},{64,96},{96,64},{128,160},{160,128},{192,224},{224,1... | collective-permute-start | bytes 221192 | tf_op jit(solution)/shard_map/ppermute | solution.py:33
  85.1 11.9 %collective-permute-start.21 = (f32[80,384]{1,0:T(8,128)S(1)}, f32[80,384]{1,0:T(8,128)S(1)}, u32[]{:S(2)}, u32[]{:S(2)}) collective-permute-start(f32[80,384]{1,0:T(8,128)S(1)} %get-tuple-element.88), channel_id=1, source_target_pairs={{0,128},{32,160},{64,192},{96,224},{128,0},{160,32},{192,64},{224,... | collective-permute-start | bytes 368648 | tf_op jit(solution)/shard_map/ppermute | solution.py:29
  92.4 8.4 %collective-permute-start.22 = (f32[80,384]{1,0:T(8,128)S(1)}, f32[80,384]{1,0:T(8,128)S(1)}, u32[]{:S(2)}, u32[]{:S(2)}) collective-permute-start(f32[80,384]{1,0:T(8,128)S(1)} %get-tuple-element.89), channel_id=1, source_target_pairs={{0,64},{32,96},{64,128},{96,160},{128,192},{160,224},{192,0},{224,... | collective-permute-start | bytes 368648 | tf_op jit(solution)/shard_map/ppermute | solution.py:29
  93.6 8.4 %collective-permute-start.23 = (f32[80,384]{1,0:T(8,128)S(1)}, f32[80,384]{1,0:T(8,128)S(1)}, u32[]{:S(2)}, u32[]{:S(2)}) collective-permute-start(f32[80,384]{1,0:T(8,128)S(1)} %get-tuple-element.87), channel_id=1, source_target_pairs={{0,192},{32,224},{64,0},{96,32},{128,64},{160,96},{192,128},{224,1... | collective-permute-start | bytes 368648 | tf_op jit(solution)/shard_map/ppermute | solution.py:29
  102.1 7.4 %collective-permute-start.28 = (f32[32,384]{1,0:T(8,128)S(1)}, f32[32,384]{1,0:T(8,128)S(1)}, u32[]{:S(2)}, u32[]{:S(2)}) collective-permute-start(f32[32,384]{1,0:T(8,128)S(1)} %slice.32), channel_id=1, source_target_pairs={{0,32},{32,0},{64,96},{96,64},{128,160},{160,128},{192,224},{224,1... | collective-permute-start | bytes 147464 | tf_op jit(solution)/shard_map/ppermute | solution.py:33
  103.1 10.8 %collective-permute-start.24 = (f32[2,48,384]{2,1,0:T(8,128)S(1)}, f32[2,48,384]{2,1,0:T(8,128)S(1)}, u32[]{:S(2)}, u32[]{:S(2)}) collective-permute-start(f32[2,48,384]{2,1,0:T(8,128)S(1)} %pad_maximum_fusion.4), channel_id=1, source_target_pairs={{0,6},{8,14},{2,0},{10,8},{4,2},{12,10},{6,4},{14,12},{1,7},{9,15}... | collective-permute-start | bytes 442376 | tf_op jit(solution)/shard_map/ppermute | solution.py:21
  105.3 9.7 %collective-permute-start.25 = (f32[2,48,384]{2,1,0:T(8,128)S(1)}, f32[2,48,384]{2,1,0:T(8,128)S(1)}, u32[]{:S(2)}, u32[]{:S(2)}) collective-permute-start(f32[2,48,384]{2,1,0:T(8,128)S(1)} %pad_maximum_fusion.4), channel_id=1, source_target_pairs={{0,4},{8,12},{2,6},{10,14},{4,0},{12,8},{6,2},{14,10},{1,5},{9,13}... | collective-permute-start | bytes 442376 | tf_op jit(solution)/shard_map/ppermute | solution.py:21
  107.0 8.1 %collective-permute-start.26 = (f32[2,48,384]{2,1,0:T(8,128)S(1)}, f32[2,48,384]{2,1,0:T(8,128)S(1)}, u32[]{:S(2)}, u32[]{:S(2)}) collective-permute-start(f32[2,48,384]{2,1,0:T(8,128)S(1)} %pad_maximum_fusion.4), channel_id=1, source_target_pairs={{0,2},{8,10},{2,4},{10,12},{4,6},{12,14},{6,0},{14,8},{1,3},{9,11}... | collective-permute-start | bytes 442376 | tf_op jit(solution)/shard_map/ppermute | solution.py:21
  109.5 7.0 %collective-permute-start.29 = (f32[64,384]{1,0:T(8,128)S(1)}, f32[64,384]{1,0:T(8,128)S(1)}, u32[]{:S(2)}, u32[]{:S(2)}) collective-permute-start(f32[64,384]{1,0:T(8,128)S(1)} %fusion.5), channel_id=1, source_target_pairs={{0,192},{32,224},{64,0},{96,32},{128,64},{160,96},{192,128},{224,1... | collective-permute-start | bytes 294920 | tf_op jit(solution)/shard_map/ppermute | solution.py:29
  112.6 9.9 %collective-permute-start.30 = (f32[64,384]{1,0:T(8,128)S(1)}, f32[64,384]{1,0:T(8,128)S(1)}, u32[]{:S(2)}, u32[]{:S(2)}) collective-permute-start(f32[64,384]{1,0:T(8,128)S(1)} %fusion.5), channel_id=1, source_target_pairs={{0,128},{32,160},{64,192},{96,224},{128,0},{160,32},{192,64},{224,... | collective-permute-start | bytes 294920 | tf_op jit(solution)/shard_map/ppermute | solution.py:29
  113.9 9.2 %collective-permute-start.31 = (f32[64,384]{1,0:T(8,128)S(1)}, f32[64,384]{1,0:T(8,128)S(1)}, u32[]{:S(2)}, u32[]{:S(2)}) collective-permute-start(f32[64,384]{1,0:T(8,128)S(1)} %fusion.5), channel_id=1, source_target_pairs={{0,64},{32,96},{64,128},{96,160},{128,192},{160,224},{192,0},{224,... | collective-permute-start | bytes 294920 | tf_op jit(solution)/shard_map/ppermute | solution.py:29
  115.2 8.7 %collective-permute-start.27 = (f32[2,192,384]{2,1,0:T(8,128)S(1)}, f32[2,192,384]{2,1,0:T(8,128)S(1)}, u32[]{:S(2)}, u32[]{:S(2)}) collective-permute-start(f32[2,192,384]{2,1,0:T(8,128)S(1)} %constant_dynamic-slice_fusion.1), channel_id=1, source_target_pairs={{0,8},{8,0},{2,10},{10,2},{4,12},{12,4},{6,14},{14,6},{1,9},{9,1},... | collective-permute-start | bytes 1769480 | tf_op jit(solution)/shard_map/ppermute | solution.py:21
where the time goes:
time: 126 us; the launch traced here: 125 us
  starting transfers between devices  59 us (47%)
  waiting for transfers between devices  34.5 us (27%)
  Pallas kernels  15.7 us (12%)
  local copies, waits for them, and re-layouts  11.5 us (9%)
  other arithmetic  2.92 us (2%)
  between operations  1.75 us (1%)
    ppermute x19, starting transfers between devices, shift(): return lax.ppermute(value, PLANE, pairs)  29.2 us
    ppermute x6, starting transfers between devices, along_pole(): return lax.ppermute(value, 'pole', [(z, (z + step) % 8) for z in range(8)])  17 us
    ppermute x19, waiting for transfers between devices, shift(): return lax.ppermute(value, PLANE, pairs)  14.7 us
    ppermute x6, waiting for transfers between devices, along_pole(): return lax.ppermute(value, 'pole', [(z, (z + step) % 8) for z in range(8)])  13.1 us
    unnamed x25, local copies, waits for them, and re-layouts  7.89 us
    pallas_call x3, Pallas kernels, next_dot(): local(next_kernel, [SMEM] + [VMEM] * 4, out_shape, count * 6 * rows * dep...  7.75 us
    ppermute x2, starting transfers between devices, panel_slot(): return lax.ppermute(value, PLANE, pairs)  7.71 us
    ppermute x3, starting transfers between devices, pole_pair(): return lax.ppermute(value, 'pole', [(z, z ^ 1) for z in range(8)])  4.99 us
  transfers between devices with their start and end apart: 32, of which 16 were waited for; matrix products, arithmetic and copies ran while one was open for 4% of the time, Pallas kernels for 9%

commit v1 on v0

--- a/solution.py
+++ b/solution.py
@@ -178,7 +178,7 @@
     return local(turn_kernel, [VMEM] * 2, out_shape, 8 * rows * width, 16 * rows * width)(own, other)
 
 
-def corr_kernel(info, p0, p1, up0, down0, up1, down1, oh, ol, th, tl, corr, sum_own, sum_other):
+def corr_kernel(info, p0, p1, up0, down0, up1, down1, oh, ol, th, tl, kept, sent, sum_own, sum_other):
     first = p0[...] + (up0[...] + down0[...])
     second = p1[...] + (up1[...] + down1[...])
     own_is_first = info[0] == 0
@@ -186,12 +186,16 @@
     others = jnp.where(own_is_first, second, first) * (info[2] > 0).astype(jnp.float32)
     sum_own[...] = mine
     sum_other[...] = others
-    corr[...] = mm3(oh[...], ol[...], *split(mine)) + mm3(th[...], tl[...], *split(others))
+    corr = mm3(oh[...], ol[...], *split(mine)) + mm3(th[...], tl[...], *split(others))
+    half = corr.shape[0] // 2
+    first_core = info[3] == 0
+    kept[...] = jnp.where(first_core, corr[:half], corr[half:])
+    sent[...] = jnp.where(first_core, corr[half:], corr[:half])
 
 
 def correction(info, *arrays):
     rows, width = arrays[0].shape
-    out_shape = [jax.ShapeDtypeStruct((n, width), jnp.float32) for n in (width, rows, rows)]
+    out_shape = [jax.ShapeDtypeStruct((n, width), jnp.float32) for n in (width // 2, width // 2, rows, rows)]
     return local(
         corr_kernel, [SMEM] + [VMEM] * len(arrays), out_shape, 12 * rows * width * width, 48 * rows * width
     )(info, *arrays)
@@ -212,6 +216,20 @@
     return local(column_kernel, [SMEM] + [VMEM] * 2, out_shape, 3 * rows * width, 16 * rows * width)(
         weight, mine, arrived
     )
+
+
+def finish_kernel(core, mine, others, diagonal, dm_diag):
+    half = mine.shape[1]
+    for side, halves in ((core[0], mine), (1 - core[0], others)):
+        at = pl.ds(pl.multiple_of(side * half, half), half)
+        diagonal[at, :] = halves[0]
+        dm_diag[at, :] = halves[1]
+
+
+def finish(core, mine, others):
+    width = mine.shape[2]
+    out_shape = [jax.ShapeDtypeStruct((width, width), jnp.float32)] * 2
+    return local(finish_kernel, [SMEM] + [VMEM] * 2, out_shape, 0, 16 * width * width)(core[None], mine, others)
 
 
 def part(value, index, size):
@@ -256,13 +274,12 @@
     info = jnp.concatenate([far, core[None], places, keep[:2]]).astype(jnp.int32)
     rest = jnp.concatenate([far, 1 - core[None], places, keep[2:4]]).astype(jnp.int32)
     straight = jnp.stack([block(1, 1), block(3, 0)]).astype(jnp.int32)
-    joined = jnp.stack([block(1, 0), block(3, 1)]).astype(jnp.int32)
-    here = jnp.stack([block(0, 0), block(0, 1)]).astype(jnp.int32)
-    tail = jnp.concatenate([x_lo[None], keep[4:]]).astype(jnp.int32)
+    joined = jnp.stack([block(1, 0), block(3, 1), block(0, 0), block(0, 1)]).astype(jnp.int32)
+    tail = jnp.concatenate([x_lo[None], keep[4:], core[None]]).astype(jnp.int32)
     dinv_part = lax.dynamic_slice_in_dim(dinv[0], core * half + y * quarter, quarter, 0)
     halves = split_inverse(ainv[0])
-    info, rest, straight, joined, here, tail, dinv_part, halves, slots = lax.optimization_barrier(
-        (info, rest, straight, joined, here, tail, dinv_part, halves, slots)
+    info, rest, straight, joined, tail, dinv_part, halves, slots = lax.optimization_barrier(
+        (info, rest, straight, joined, tail, dinv_part, halves, slots)
     )
     others = [sibling(s) for s in slots]
 
@@ -271,10 +288,9 @@
     up, down = shift(up, dy=1), shift(down, dy=-1)
     p11, p30 = next_dot(straight, halves, panel, rows, 2)
     up1, down0 = shift(p11, dy=1), shift(p30, dy=-1)
-    p10, p31 = next_dot(joined, halves, panel, rows, 2)
+    p10, p31, p00, p01 = next_dot(joined, halves, panel, rows, 4)
     up0, down1 = shift(p10 + up, dy=1), shift(p31 + down, dy=-1)
-    p00, p01 = next_dot(here, halves, panel, rows, 2)
-    corr, sum_own, sum_other = correction(tail, p00, p01, up0, down0, up1, down1, *turned(own, flip_x(own)))
+    kept, sent, sum_own, sum_other = correction(tail, p00, p01, up0, down0, up1, down1, *turned(own, flip_x(own)))
 
     pair, four = z % 2, z // 2
     eighth, middle = rows // 8, rows // 2
@@ -282,7 +298,7 @@
     dm = part(weighted, pair, middle) + pole_pair(part(weighted, 1 - pair, middle))
 
     steps = (1, 2, 3)
-    mine = part(corr, core, half) + sibling(part(corr, 1 - core, half))
+    mine = kept + sibling(sent)
     away = [shift(part(mine, (y + k) % 4, quarter), dy=k) for k in steps]
     mine = (part(mine, y, quarter) + away[1]) + (away[0] + away[2])
     away = [shift(mine, dx=k) for k in steps]
@@ -295,12 +311,12 @@
 
     both = jnp.stack([diagonal, summed[eighth:]])
     both = in_ring_order(both, [shift(both, dy=k) for k in steps], y, 1)
-    both = in_pair_order(both, sibling(both), core, 1)
+    diagonal, dm_diag = finish(core, both, sibling(both))
     dm = summed[:eighth]
     dm = in_pair_order(dm, pole_pair(dm), pair)
     dm = in_ring_order(dm, [along_pole(dm, 2 * k) for k in steps], four)
 
-    return column[None], both[:1], dm, both[1]
+    return column[None], diagonal[None], dm, dm_diag
 
 
 def solution(mesh):

time: 126 us -> 124 us (0.984)
  waiting for transfers between devices: 34.5 us -> 41.4 us
  local copies, waits for them, and re-layouts: 11.5 us -> 5.99 us
  other arithmetic: 2.92 us -> 0.99 us
    ppermute x19, waiting for transfers between devices: 14.7 us -> 21.6 us  [shift(): return lax.ppermute(value, PLANE, pairs)]
    unnamed x25 -> x17, local copies, waits for them, and re-layouts: 7.89 us -> 3.51 us
    add x2, other arithmetic: 1.6 us -> 0.12 us  [on_device(): up0, down1 = (shift(p10 + up, dy=1), shift(p31 + down, dy=-1))]
    pallas_call x3 -> x2, Pallas kernels: 7.75 us -> 6.38 us  [next_dot(): local(next_kernel, [SMEM] + [VMEM] * 4, out_shape, count * 6 * rows * dep...]
  transfers between devices with their start and end apart: 32 -> 32, of which waited for: 16 -> 19; matrix products, arithmetic and copies ran while one was open for 4% -> 3% of each run, Pallas kernels for 9% -> 8%
where the time goes in v1:
time: 124 us
  starting transfers between devices  59.4 us (48%)
  waiting for transfers between devices  41.4 us (33%)
  Pallas kernels  14.7 us (12%)
  local copies, waits for them, and re-layouts  5.99 us (5%)
  between operations  1.69 us (1%)
    ppermute x19, starting transfers between devices, shift(): return lax.ppermute(value, PLANE, pairs)  29.6 us
    ppermute x19, waiting for transfers between devices, shift(): return lax.ppermute(value, PLANE, pairs)  21.6 us
    ppermute x6, starting transfers between devices, along_pole(): return lax.ppermute(value, 'pole', [(z, (z + step) % 8) for z in range(8)])  17 us
    ppermute x6, waiting for transfers between devices, along_pole(): return lax.ppermute(value, 'pole', [(z, (z + step) % 8) for z in range(8)])  13.1 us
    ppermute x2, starting transfers between devices, panel_slot(): return lax.ppermute(value, PLANE, pairs)  7.71 us
    pallas_call x2, Pallas kernels, next_dot(): local(next_kernel, [SMEM] + [VMEM] * 4, out_shape, count * 6 * rows * dep...  6.38 us
    ppermute x3, starting transfers between devices, pole_pair(): return lax.ppermute(value, 'pole', [(z, z ^ 1) for z in range(8)])  4.99 us
    ppermute x2, waiting for transfers between devices, panel_slot(): return lax.ppermute(value, PLANE, pairs)  3.67 us
  transfers between devices with their start and end apart: 32, of which 19 were waited for; matrix products, arithmetic and copies ran while one was open for 3% of the time, Pallas kernels for 8%

profile of v1, /device:TPU:8, one launch (start us, length us, event | category | flops | bytes accessed | tf_op | source)
XLA Modules:
  0.0 124.2 jit_solution(1730383411669633496)
XLA Ops:
  0.6 2.1 %collective-permute-start = (f32[256,384]{1,0:T(8,128)}, f32[256,384]{1,0:T(8,128)S(1)}, u32[]{:S(2)}, u32[]{:S(2)}) collective-permute-start(f32[256,384]{1,0:T(8,128)} %bitcast.36), channel_id=1, source_target_pairs={{0,0},{2,8},{8,2},{10,10},{16,4},{18,12},{24,6},{26,14},{4,1},{6,9... | collective-permute-start | bytes 1179656 | tf_op jit(solution)/shard_map/ppermute | solution.py:42
  2.7 5.7 %collective-permute-start.1 = (f32[256,384]{1,0:T(8,128)}, f32[256,384]{1,0:T(8,128)S(1)}, u32[]{:S(2)}, u32[]{:S(2)}) collective-permute-start(f32[256,384]{1,0:T(8,128)} %bitcast.37), channel_id=1, source_target_pairs={{1,0},{3,8},{9,2},{11,10},{17,4},{19,12},{25,6},{27,14},{5,1},{7,9... | collective-permute-start | bytes 1179656 | tf_op jit(solution)/shard_map/ppermute | solution.py:42
  8.8 1.3 %gather_fusion = s32[6]{0:T(128)S(1)} fusion(s32[32]{0:T(128)} %param.9, s32[1024]{0:T(1024)S(1)} %pad_clamp_fusion), kind=kCustom, calls=%fused_computation | custom fusion | bytes 72 | tf_op jit(solution)/shard_map/jit(_take)/gather | solution.py:267
  10.4 3.4 %copy-done.1 = f32[1,2048,1024]{2,1,0:T(8,128)S(1)} copy-done((f32[1,2048,1024]{2,1,0:T(8,128)S(1)}, f32[1,2048,1024]{2,1,0:T(8,128)}, u32[]{:S(2)}) %copy-start.1) | copy-done | bytes 8388632
  13.8 1.1 shard_map.84
  15.1 3.7 %collective-permute-done.s0 = f32[256,384]{1,0:T(8,128)S(1)} collective-permute-done((f32[256,384]{1,0:T(8,128)}, f32[256,384]{1,0:T(8,128)S(1)}, u32[]{:S(2)}, u32[]{:S(2)}) %collective-permute-start) | collective-permute-done | bytes 393248 | tf_op jit(solution)/shard_map/ppermute | solution.py:42
  19.3 1.7 %shard_map.85 = (f32[256,384]{1,0:T(8,128)S(1)}, f32[256,384]{1,0:T(8,128)S(1)}, bf16[512,384]{1,0:T(8,128)(2,1)S(1)}, bf16[512,384]{1,0:T(8,128)(2,1)S(1)}) custom-call(s32[7]{0:T(128)S(1)} %concatenate.90.info, f32[256,384]{1,0:T(8,128)S(1)} %collective-permute-done.s0, f32[256,384]{1,0:T(8,128)S(1)} %collective-permute-done.1.s1, ...), custom_call_target="tpu_custom_call" | custom-call | flops 603979776 | bytes 3407872 | tf_op jit(solution)/shard_map/pallas_call | solution.py:138
  21.1 1.9 %shard_map.86 = (f32[256,384]{1,0:T(8,128)S(1)}, f32[256,384]{1,0:T(8,128)S(1)}, bf16[1024,384]{1,0:T(8,128)(2,1)S(1)}, bf16[1024,384]{1,0:T(8,128)(2,1)S(1)}) custom-call(s32[7]{0:T(128)S(1)} %concatenate.91.info, f32[256,384]{1,0:T(8,128)S(1)} %collective-permute-done.2.t0, f32[256,384]{1,0:T(8,128)S(1)} %collective-permute-done.3.t1, ...), custom_call_target="tpu_custom_call" | custom-call | flops 603979776 | bytes 4980736 | tf_op jit(solution)/shard_map/pallas_call | solution.py:148
  23.6 8.8 %collective-permute-start.4 = (f32[256,384]{1,0:T(8,128)S(1)}, f32[256,384]{1,0:T(8,128)S(1)}, u32[]{:S(2)}, u32[]{:S(2)}) collective-permute-start(f32[256,384]{1,0:T(8,128)S(1)} %get-tuple-element.61), channel_id=1, source_target_pairs={{0,2},{8,10},{2,4},{10,12},{4,6},{12,14},{6,0},{14,8},{1,3},{9,11}... | collective-permute-start | bytes 1179656 | tf_op jit(solution)/shard_map/ppermute | solution.py:21
  32.4 2.4 %shard_map.88 = (f32[256,384]{1,0:T(8,128)S(1)}, f32[256,384]{1,0:T(8,128)S(1)}) custom-call(s32[2]{0:T(128)S(1)} %pad_add_fusion.info, bf16[1024,384]{1,0:T(8,128)(2,1)S(1)} %get-tuple-element.56.high, bf16[1024,384]{1,0:T(8,128)(2,1)S(1)} %get-tuple-element.57.low, bf16[2048,1024]{1,0:T(8,128)(2,1)S(1)} %get-tuple-element.50.a_high, ...), custom_call_target="tpu_custom_call" | custom-call | flops 1207959552 | bytes 2883584 | tf_op jit(solution)/shard_map/pallas_call | solution.py:161
  34.8 1.7 %collective-permute-start.6 = (f32[256,384]{1,0:T(8,128)S(1)}, f32[256,384]{1,0:T(8,128)S(1)}, u32[]{:S(2)}, u32[]{:S(2)}) collective-permute-start(f32[256,384]{1,0:T(8,128)S(1)} %get-tuple-element.63), channel_id=1, source_target_pairs={{0,6},{8,14},{2,0},{10,8},{4,2},{12,10},{6,4},{14,12},{1,7},{9,15}... | collective-permute-start | bytes 1179656 | tf_op jit(solution)/shard_map/ppermute | solution.py:21
  37.1 4.0 %shard_map.87 = (f32[256,384]{1,0:T(8,128)S(1)}, f32[256,384]{1,0:T(8,128)S(1)}, f32[256,384]{1,0:T(8,128)S(1)}, f32[256,384]{1,0:T(8,128)S(1)}) custom-call(s32[4]{0:T(128)S(1)} %get-tuple-element.45.info, bf16[1024,384]{1,0:T(8,128)(2,1)S(1)} %get-tuple-element.56.high, bf16[1024,384]{1,0:T(8,128)(2,1)S(1)} %get-tuple-element.57.low, ...), custom_call_target="tpu_custom_call" | custom-call | flops 2415919104 | bytes 5767168 | tf_op jit(solution)/shard_map/pallas_call | solution.py:161
  41.1 1.1 collective-permute-done.8
  42.3 1.6 %collective-permute-start.9 = (f32[256,384]{1,0:T(8,128)S(1)}, f32[256,384]{1,0:T(8,128)S(1)}, u32[]{:S(2)}, u32[]{:S(2)}) collective-permute-start(f32[256,384]{1,0:T(8,128)S(1)} %add.256), channel_id=1, source_target_pairs={{0,6},{8,14},{2,0},{10,8},{4,2},{12,10},{6,4},{14,12},{1,7},{9,15}... | collective-permute-start | bytes 1179656 | tf_op jit(solution)/shard_map/ppermute | solution.py:21
  44.9 5.8 %collective-permute-done.6.down0 = f32[256,384]{1,0:T(8,128)S(1)} collective-permute-done((f32[256,384]{1,0:T(8,128)S(1)}, f32[256,384]{1,0:T(8,128)S(1)}, u32[]{:S(2)}, u32[]{:S(2)}) %collective-permute-start.6) | collective-permute-done | bytes 393248 | tf_op jit(solution)/shard_map/ppermute | solution.py:21
  50.6 1.7 %collective-permute-done.7.up1 = f32[256,384]{1,0:T(8,128)S(1)} collective-permute-done((f32[256,384]{1,0:T(8,128)S(1)}, f32[256,384]{1,0:T(8,128)S(1)}, u32[]{:S(2)}, u32[]{:S(2)}) %collective-permute-start.7) | collective-permute-done | bytes 393248 | tf_op jit(solution)/shard_map/ppermute | solution.py:21
  52.4 6.2 %collective-permute-done.9.down1 = f32[256,384]{1,0:T(8,128)S(1)} collective-permute-done((f32[256,384]{1,0:T(8,128)S(1)}, f32[256,384]{1,0:T(8,128)S(1)}, u32[]{:S(2)}, u32[]{:S(2)}) %collective-permute-start.9) | collective-permute-done | bytes 393248 | tf_op jit(solution)/shard_map/ppermute | solution.py:21
  58.6 1.4 %collective-permute-done.5.up0 = f32[256,384]{1,0:T(8,128)S(1)} collective-permute-done((f32[256,384]{1,0:T(8,128)S(1)}, f32[256,384]{1,0:T(8,128)S(1)}, u32[]{:S(2)}, u32[]{:S(2)}) %collective-permute-start.5) | collective-permute-done | bytes 393248 | tf_op jit(solution)/shard_map/ppermute | solution.py:21
  60.0 1.5 %shard_map.90 = (f32[192,384]{1,0:T(8,128)S(1)}, f32[192,384]{1,0:T(8,128)S(1)}, f32[256,384]{1,0:T(8,128)S(1)}, f32[256,384]{1,0:T(8,128)S(1)}) custom-call(s32[4]{0:T(128)S(1)} %get-tuple-element.44.info, f32[256,384]{1,0:T(8,128)S(1)} %get-tuple-element.58.p0, f32[256,384]{1,0:T(8,128)S(1)} %get-tuple-element.59.p1, ...), custom_call_target="tpu_custom_call" | custom-call | flops 452984832 | bytes 4718592 | tf_op jit(solution)/shard_map/pallas_call | solution.py:199
  61.7 1.4 %collective-permute-done.12 = f32[192,384]{1,0:T(8,128)S(1)} collective-permute-done((f32[192,384]{1,0:T(8,128)S(1)}, f32[192,384]{1,0:T(8,128)S(1)}, u32[]{:S(2)}, u32[]{:S(2)}) %collective-permute-start.12) | collective-permute-done | bytes 294944 | tf_op jit(solution)/shard_map/ppermute | solution.py:21
  63.2 2.2 %collective-permute-start.13 = (f32[48,384]{1,0:T(8,128)S(1)}, f32[48,384]{1,0:T(8,128)S(1)}, u32[]{:S(2)}, u32[]{:S(2)}) collective-permute-start(f32[48,384]{1,0:T(8,128)S(1)} %get-tuple-element.82), channel_id=1, source_target_pairs={{0,4},{8,12},{2,6},{10,14},{4,0},{12,8},{6,2},{14,10},{1,5},{9,13}... | collective-permute-start | bytes 221192 | tf_op jit(solution)/shard_map/ppermute | solution.py:21
  65.4 2.3 %collective-permute-start.14 = (f32[48,384]{1,0:T(8,128)S(1)}, f32[48,384]{1,0:T(8,128)S(1)}, u32[]{:S(2)}, u32[]{:S(2)}) collective-permute-start(f32[48,384]{1,0:T(8,128)S(1)} %get-tuple-element.84), channel_id=1, source_target_pairs={{0,2},{8,10},{2,4},{10,12},{4,6},{12,14},{6,0},{14,8},{1,3},{9,11}... | collective-permute-start | bytes 221192 | tf_op jit(solution)/shard_map/ppermute | solution.py:21
  68.4 0.8 collective-permute-done.13
  69.1 1.2 %collective-permute-done.14 = f32[48,384]{1,0:T(8,128)S(1)} collective-permute-done((f32[48,384]{1,0:T(8,128)S(1)}, f32[48,384]{1,0:T(8,128)S(1)}, u32[]{:S(2)}, u32[]{:S(2)}) %collective-permute-start.14) | collective-permute-done | bytes 73760 | tf_op jit(solution)/shard_map/ppermute | solution.py:21
  70.4 1.7 %collective-permute-done.15 = f32[48,384]{1,0:T(8,128)S(1)} collective-permute-done((f32[48,384]{1,0:T(8,128)S(1)}, f32[48,384]{1,0:T(8,128)S(1)}, u32[]{:S(2)}, u32[]{:S(2)}) %collective-permute-start.15) | collective-permute-done | bytes 73760 | tf_op jit(solution)/shard_map/ppermute | solution.py:21
  72.1 0.9 collective-permute-start.16
  72.9 0.8 collective-permute-start.17
  73.8 2.4 %collective-permute-start.18 = (f32[48,384]{1,0:T(8,128)S(1)}, f32[48,384]{1,0:T(8,128)S(1)}, u32[]{:S(2)}, u32[]{:S(2)}) collective-permute-start(f32[48,384]{1,0:T(8,128)S(1)} %add_add_fusion.1), channel_id=1, source_target_pairs={{0,17},{8,25},{2,19},{10,27},{4,21},{12,29},{6,23},{14,31},{1,0},{... | collective-permute-start | bytes 221192 | tf_op jit(solution)/shard_map/ppermute | solution.py:21
  76.2 0.8 shard_map.91
  77.0 2.0 %collective-permute-start.19 = (f32[128,384]{1,0:T(8,128)S(1)}, f32[128,384]{1,0:T(8,128)S(1)}, u32[]{:S(2)}, u32[]{:S(2)}) collective-permute-start(f32[128,384]{1,0:T(8,128)S(1)} %constant_dynamic-slice_fusion.6), channel_id=1, source_target_pairs={{0,32},{32,0},{64,96},{96,64},{128,160},{160,128},{192,224},{224,1... | collective-permute-start | bytes 589832 | tf_op jit(solution)/shard_map/ppermute | solution.py:33
  79.0 2.0 %collective-permute-start.20 = (f32[48,384]{1,0:T(8,128)S(1)}, f32[48,384]{1,0:T(8,128)S(1)}, u32[]{:S(2)}, u32[]{:S(2)}) collective-permute-start(f32[48,384]{1,0:T(8,128)S(1)} %get-tuple-element.80), channel_id=1, source_target_pairs={{0,32},{32,0},{64,96},{96,64},{128,160},{160,128},{192,224},{224,1... | collective-permute-start | bytes 221192 | tf_op jit(solution)/shard_map/ppermute | solution.py:33
  81.1 3.1 %collective-permute-done.20 = f32[48,384]{1,0:T(8,128)S(1)} collective-permute-done((f32[48,384]{1,0:T(8,128)S(1)}, f32[48,384]{1,0:T(8,128)S(1)}, u32[]{:S(2)}, u32[]{:S(2)}) %collective-permute-start.20) | collective-permute-done | bytes 73760 | tf_op jit(solution)/shard_map/ppermute | solution.py:33
  84.2 7.4 %collective-permute-start.21 = (f32[80,384]{1,0:T(8,128)S(1)}, f32[80,384]{1,0:T(8,128)S(1)}, u32[]{:S(2)}, u32[]{:S(2)}) collective-permute-start(f32[80,384]{1,0:T(8,128)S(1)} %get-tuple-element.90), channel_id=1, source_target_pairs={{0,128},{32,160},{64,192},{96,224},{128,0},{160,32},{192,64},{224,... | collective-permute-start | bytes 368648 | tf_op jit(solution)/shard_map/ppermute | solution.py:29
  91.6 1.2 collective-permute-start.22
  92.8 2.9 %collective-permute-start.23 = (f32[80,384]{1,0:T(8,128)S(1)}, f32[80,384]{1,0:T(8,128)S(1)}, u32[]{:S(2)}, u32[]{:S(2)}) collective-permute-start(f32[80,384]{1,0:T(8,128)S(1)} %get-tuple-element.89), channel_id=1, source_target_pairs={{0,192},{32,224},{64,0},{96,32},{128,64},{160,96},{192,128},{224,1... | collective-permute-start | bytes 368648 | tf_op jit(solution)/shard_map/ppermute | solution.py:29
  96.2 3.9 %collective-permute-done.22 = f32[80,384]{1,0:T(8,128)S(1)} collective-permute-done((f32[80,384]{1,0:T(8,128)S(1)}, f32[80,384]{1,0:T(8,128)S(1)}, u32[]{:S(2)}, u32[]{:S(2)}) %collective-permute-start.22) | collective-permute-done | bytes 122912 | tf_op jit(solution)/shard_map/ppermute | solution.py:29
  100.0 1.2 collective-permute-done.23
  101.3 0.9 collective-permute-start.28
  102.2 2.2 %collective-permute-start.24 = (f32[2,48,384]{2,1,0:T(8,128)S(1)}, f32[2,48,384]{2,1,0:T(8,128)S(1)}, u32[]{:S(2)}, u32[]{:S(2)}) collective-permute-start(f32[2,48,384]{2,1,0:T(8,128)S(1)} %pad_maximum_fusion.4), channel_id=1, source_target_pairs={{0,6},{8,14},{2,0},{10,8},{4,2},{12,10},{6,4},{14,12},{1,7},{9,15}... | collective-permute-start | bytes 442376 | tf_op jit(solution)/shard_map/ppermute | solution.py:21
  104.5 1.7 %collective-permute-start.25 = (f32[2,48,384]{2,1,0:T(8,128)S(1)}, f32[2,48,384]{2,1,0:T(8,128)S(1)}, u32[]{:S(2)}, u32[]{:S(2)}) collective-permute-start(f32[2,48,384]{2,1,0:T(8,128)S(1)} %pad_maximum_fusion.4), channel_id=1, source_target_pairs={{0,4},{8,12},{2,6},{10,14},{4,0},{12,8},{6,2},{14,10},{1,5},{9,13}... | collective-permute-start | bytes 442376 | tf_op jit(solution)/shard_map/ppermute | solution.py:21
  106.2 2.5 %collective-permute-start.26 = (f32[2,48,384]{2,1,0:T(8,128)S(1)}, f32[2,48,384]{2,1,0:T(8,128)S(1)}, u32[]{:S(2)}, u32[]{:S(2)}) collective-permute-start(f32[2,48,384]{2,1,0:T(8,128)S(1)} %pad_maximum_fusion.4), channel_id=1, source_target_pairs={{0,2},{8,10},{2,4},{10,12},{4,6},{12,14},{6,0},{14,8},{1,3},{9,11}... | collective-permute-start | bytes 442376 | tf_op jit(solution)/shard_map/ppermute | solution.py:21
  108.7 3.0 %collective-permute-start.29 = (f32[64,384]{1,0:T(8,128)S(1)}, f32[64,384]{1,0:T(8,128)S(1)}, u32[]{:S(2)}, u32[]{:S(2)}) collective-permute-start(f32[64,384]{1,0:T(8,128)S(1)} %fusion.3), channel_id=1, source_target_pairs={{0,192},{32,224},{64,0},{96,32},{128,64},{160,96},{192,128},{224,1... | collective-permute-start | bytes 294920 | tf_op jit(solution)/shard_map/ppermute | solution.py:29
  111.8 1.3 %collective-permute-start.30 = (f32[64,384]{1,0:T(8,128)S(1)}, f32[64,384]{1,0:T(8,128)S(1)}, u32[]{:S(2)}, u32[]{:S(2)}) collective-permute-start(f32[64,384]{1,0:T(8,128)S(1)} %fusion.3), channel_id=1, source_target_pairs={{0,128},{32,160},{64,192},{96,224},{128,0},{160,32},{192,64},{224,... | collective-permute-start | bytes 294920 | tf_op jit(solution)/shard_map/ppermute | solution.py:29
  113.1 1.1 collective-permute-start.31
  114.5 1.2 collective-permute-done.29
  115.7 5.9 %collective-permute-done.30 = f32[64,384]{1,0:T(8,128)S(1)} collective-permute-done((f32[64,384]{1,0:T(8,128)S(1)}, f32[64,384]{1,0:T(8,128)S(1)}, u32[]{:S(2)}, u32[]{:S(2)}) %collective-permute-start.30) | collective-permute-done | bytes 98336 | tf_op jit(solution)/shard_map/ppermute | solution.py:29
  122.3 0.8 constant_dynamic-slice_fusion
  123.1 1.1 shard_map.92
  (77 shorter events, 5.5 us)
Async XLA Ops:
  0.6 14.5 %copy-start = (f32[1,384,384]{2,1,0:T(8,128)S(1)}, f32[1,384,384]{2,1,0:T(8,128)}, u32[]{:S(2)}) copy-start(f32[1,384,384]{2,1,0:T(8,128)} %param.7) | copy-start | bytes 1769476
  0.6 18.1 %collective-permute-start = (f32[256,384]{1,0:T(8,128)}, f32[256,384]{1,0:T(8,128)S(1)}, u32[]{:S(2)}, u32[]{:S(2)}) collective-permute-start(f32[256,384]{1,0:T(8,128)} %bitcast.36), channel_id=1, source_target_pairs={{0,0},{2,8},{8,2},{10,10},{16,4},{18,12},{24,6},{26,14},{4,1},{6,9... | collective-permute-start | bytes 1179656 | tf_op jit(solution)/shard_map/ppermute | solution.py:42
  2.7 16.1 %collective-permute-start.1 = (f32[256,384]{1,0:T(8,128)}, f32[256,384]{1,0:T(8,128)S(1)}, u32[]{:S(2)}, u32[]{:S(2)}) collective-permute-start(f32[256,384]{1,0:T(8,128)} %bitcast.37), channel_id=1, source_target_pairs={{1,0},{3,8},{9,2},{11,10},{17,4},{19,12},{25,6},{27,14},{5,1},{7,9... | collective-permute-start | bytes 1179656 | tf_op jit(solution)/shard_map/ppermute | solution.py:42
  10.4 3.4 %copy-start.1 = (f32[1,2048,1024]{2,1,0:T(8,128)S(1)}, f32[1,2048,1024]{2,1,0:T(8,128)}, u32[]{:S(2)}) copy-start(f32[1,2048,1024]{2,1,0:T(8,128)} %param.5) | copy-start | bytes 25165828
  18.8 2.2 %collective-permute-start.2 = (f32[256,384]{1,0:T(8,128)S(1)}, f32[256,384]{1,0:T(8,128)S(1)}, u32[]{:S(2)}, u32[]{:S(2)}) collective-permute-start(f32[256,384]{1,0:T(8,128)S(1)} %collective-permute-done.s0), channel_id=1, source_target_pairs={{0,8},{8,0},{2,10},{10,2},{4,12},{12,4},{6,14},{14,6},{1,9},{9,1},... | collective-permute-start | bytes 1179656 | tf_op jit(solution)/shard_map/ppermute | solution.py:21
  18.8 2.3 %collective-permute-start.3 = (f32[256,384]{1,0:T(8,128)S(1)}, f32[256,384]{1,0:T(8,128)S(1)}, u32[]{:S(2)}, u32[]{:S(2)}) collective-permute-start(f32[256,384]{1,0:T(8,128)S(1)} %collective-permute-done.1.s1), channel_id=1, source_target_pairs={{0,8},{8,0},{2,10},{10,2},{4,12},{12,4},{6,14},{14,6},{1,9},{9,1},... | collective-permute-start | bytes 1179656 | tf_op jit(solution)/shard_map/ppermute | solution.py:21
  21.1 11.3 %copy-start.2 = (f32[1,256,384]{2,1,0:T(8,128)S(1)}, f32[1,256,384]{2,1,0:T(8,128)}, u32[]{:S(2)}) copy-start(f32[1,256,384]{2,1,0:T(8,128)} %param.6) | copy-start | bytes 1179652
  23.0 19.2 %collective-permute-start.8 = (f32[256,384]{1,0:T(8,128)S(1)}, f32[256,384]{1,0:T(8,128)S(1)}, u32[]{:S(2)}, u32[]{:S(2)}) collective-permute-start(f32[256,384]{1,0:T(8,128)S(1)} %get-tuple-element.66), channel_id=1, source_target_pairs={{0,6},{8,14},{2,0},{10,8},{4,2},{12,10},{6,4},{14,12},{1,7},{9,15}... | collective-permute-start | bytes 1179656 | tf_op jit(solution)/shard_map/ppermute | solution.py:21
  23.6 20.3 %collective-permute-start.4 = (f32[256,384]{1,0:T(8,128)S(1)}, f32[256,384]{1,0:T(8,128)S(1)}, u32[]{:S(2)}, u32[]{:S(2)}) collective-permute-start(f32[256,384]{1,0:T(8,128)S(1)} %get-tuple-element.61), channel_id=1, source_target_pairs={{0,2},{8,10},{2,4},{10,12},{4,6},{12,14},{6,0},{14,8},{1,3},{9,11}... | collective-permute-start | bytes 1179656 | tf_op jit(solution)/shard_map/ppermute | solution.py:21
  32.4 12.2 %collective-permute-start.10 = (f32[256,384]{1,0:T(8,128)S(1)}, f32[256,384]{1,0:T(8,128)S(1)}, u32[]{:S(2)}, u32[]{:S(2)}) collective-permute-start(f32[256,384]{1,0:T(8,128)S(1)} %bitcast.38), channel_id=1, source_target_pairs={{0,1},{8,9},{2,3},{10,11},{4,5},{12,13},{6,7},{14,15},{1,0},{9,8},... | collective-permute-start | bytes 1179656 | tf_op jit(solution)/shard_map/ppermute | solution.py:25
  34.8 15.9 %collective-permute-start.6 = (f32[256,384]{1,0:T(8,128)S(1)}, f32[256,384]{1,0:T(8,128)S(1)}, u32[]{:S(2)}, u32[]{:S(2)}) collective-permute-start(f32[256,384]{1,0:T(8,128)S(1)} %get-tuple-element.63), channel_id=1, source_target_pairs={{0,6},{8,14},{2,0},{10,8},{4,2},{12,10},{6,4},{14,12},{1,7},{9,15}... | collective-permute-start | bytes 1179656 | tf_op jit(solution)/shard_map/ppermute | solution.py:21
  36.5 15.9 %collective-permute-start.7 = (f32[256,384]{1,0:T(8,128)S(1)}, f32[256,384]{1,0:T(8,128)S(1)}, u32[]{:S(2)}, u32[]{:S(2)}) collective-permute-start(f32[256,384]{1,0:T(8,128)S(1)} %get-tuple-element.64), channel_id=1, source_target_pairs={{0,2},{8,10},{2,4},{10,12},{4,6},{12,14},{6,0},{14,8},{1,3},{9,11}... | collective-permute-start | bytes 1179656 | tf_op jit(solution)/shard_map/ppermute | solution.py:21
  42.3 16.3 %collective-permute-start.9 = (f32[256,384]{1,0:T(8,128)S(1)}, f32[256,384]{1,0:T(8,128)S(1)}, u32[]{:S(2)}, u32[]{:S(2)}) collective-permute-start(f32[256,384]{1,0:T(8,128)S(1)} %add.256), channel_id=1, source_target_pairs={{0,6},{8,14},{2,0},{10,8},{4,2},{12,10},{6,4},{14,12},{1,7},{9,15}... | collective-permute-start | bytes 1179656 | tf_op jit(solution)/shard_map/ppermute | solution.py:21
  44.0 16.0 %collective-permute-start.5 = (f32[256,384]{1,0:T(8,128)S(1)}, f32[256,384]{1,0:T(8,128)S(1)}, u32[]{:S(2)}, u32[]{:S(2)}) collective-permute-start(f32[256,384]{1,0:T(8,128)S(1)} %add.255), channel_id=1, source_target_pairs={{0,2},{8,10},{2,4},{10,12},{4,6},{12,14},{6,0},{14,8},{1,3},{9,11}... | collective-permute-start | bytes 1179656 | tf_op jit(solution)/shard_map/ppermute | solution.py:21
  61.5 1.7 %collective-permute-start.12 = (f32[192,384]{1,0:T(8,128)S(1)}, f32[192,384]{1,0:T(8,128)S(1)}, u32[]{:S(2)}, u32[]{:S(2)}) collective-permute-start(f32[192,384]{1,0:T(8,128)S(1)} %get-tuple-element.76), channel_id=1, source_target_pairs={{0,8},{8,0},{2,10},{10,2},{4,12},{12,4},{6,14},{14,6},{1,9},{9,1},... | collective-permute-start | bytes 884744 | tf_op jit(solution)/shard_map/ppermute | solution.py:21
  61.6 14.6 %collective-permute-start.11 = (f32[256,384]{1,0:T(8,128)S(1)}, f32[256,384]{1,0:T(8,128)S(1)}, u32[]{:S(2)}, u32[]{:S(2)}) collective-permute-start(f32[256,384]{1,0:T(8,128)S(1)} %get-tuple-element.72), channel_id=1, source_target_pairs={{0,1},{8,9},{2,3},{10,11},{4,5},{12,13},{6,7},{14,15},{1,0},{9,8},... | collective-permute-start | bytes 1179656 | tf_op jit(solution)/shard_map/ppermute | solution.py:25
  63.2 5.9 %collective-permute-start.13 = (f32[48,384]{1,0:T(8,128)S(1)}, f32[48,384]{1,0:T(8,128)S(1)}, u32[]{:S(2)}, u32[]{:S(2)}) collective-permute-start(f32[48,384]{1,0:T(8,128)S(1)} %get-tuple-element.82), channel_id=1, source_target_pairs={{0,4},{8,12},{2,6},{10,14},{4,0},{12,8},{6,2},{14,10},{1,5},{9,13}... | collective-permute-start | bytes 221192 | tf_op jit(solution)/shard_map/ppermute | solution.py:21
  65.4 5.0 %collective-permute-start.14 = (f32[48,384]{1,0:T(8,128)S(1)}, f32[48,384]{1,0:T(8,128)S(1)}, u32[]{:S(2)}, u32[]{:S(2)}) collective-permute-start(f32[48,384]{1,0:T(8,128)S(1)} %get-tuple-element.84), channel_id=1, source_target_pairs={{0,2},{8,10},{2,4},{10,12},{4,6},{12,14},{6,0},{14,8},{1,3},{9,11}... | collective-permute-start | bytes 221192 | tf_op jit(solution)/shard_map/ppermute | solution.py:21
  67.7 4.4 %collective-permute-start.15 = (f32[48,384]{1,0:T(8,128)S(1)}, f32[48,384]{1,0:T(8,128)S(1)}, u32[]{:S(2)}, u32[]{:S(2)}) collective-permute-start(f32[48,384]{1,0:T(8,128)S(1)} %get-tuple-element.83), channel_id=1, source_target_pairs={{0,6},{8,14},{2,0},{10,8},{4,2},{12,10},{6,4},{14,12},{1,7},{9,15}... | collective-permute-start | bytes 221192 | tf_op jit(solution)/shard_map/ppermute | solution.py:21
  72.1 6.9 %collective-permute-start.16 = (f32[48,384]{1,0:T(8,128)S(1)}, f32[48,384]{1,0:T(8,128)S(1)}, u32[]{:S(2)}, u32[]{:S(2)}) collective-permute-start(f32[48,384]{1,0:T(8,128)S(1)} %add_add_fusion.1), channel_id=1, source_target_pairs={{0,16},{8,24},{2,18},{10,26},{4,20},{12,28},{6,22},{14,30},{1,17},... | collective-permute-start | bytes 221192 | tf_op jit(solution)/shard_map/ppermute | solution.py:21
  72.9 6.1 %collective-permute-start.17 = (f32[48,384]{1,0:T(8,128)S(1)}, f32[48,384]{1,0:T(8,128)S(1)}, u32[]{:S(2)}, u32[]{:S(2)}) collective-permute-start(f32[48,384]{1,0:T(8,128)S(1)} %add_add_fusion.1), channel_id=1, source_target_pairs={{0,1},{8,9},{2,3},{10,11},{4,5},{12,13},{6,7},{14,15},{1,16},{9,24... | collective-permute-start | bytes 221192 | tf_op jit(solution)/shard_map/ppermute | solution.py:21
  73.8 5.2 %collective-permute-start.18 = (f32[48,384]{1,0:T(8,128)S(1)}, f32[48,384]{1,0:T(8,128)S(1)}, u32[]{:S(2)}, u32[]{:S(2)}) collective-permute-start(f32[48,384]{1,0:T(8,128)S(1)} %add_add_fusion.1), channel_id=1, source_target_pairs={{0,17},{8,25},{2,19},{10,27},{4,21},{12,29},{6,23},{14,31},{1,0},{... | collective-permute-start | bytes 221192 | tf_op jit(solution)/shard_map/ppermute | solution.py:21
  77.0 7.2 %collective-permute-start.19 = (f32[128,384]{1,0:T(8,128)S(1)}, f32[128,384]{1,0:T(8,128)S(1)}, u32[]{:S(2)}, u32[]{:S(2)}) collective-permute-start(f32[128,384]{1,0:T(8,128)S(1)} %constant_dynamic-slice_fusion.6), channel_id=1, source_target_pairs={{0,32},{32,0},{64,96},{96,64},{128,160},{160,128},{192,224},{224,1... | collective-permute-start | bytes 589832 | tf_op jit(solution)/shard_map/ppermute | solution.py:33
  79.0 5.1 %collective-permute-start.20 = (f32[48,384]{1,0:T(8,128)S(1)}, f32[48,384]{1,0:T(8,128)S(1)}, u32[]{:S(2)}, u32[]{:S(2)}) collective-permute-start(f32[48,384]{1,0:T(8,128)S(1)} %get-tuple-element.80), channel_id=1, source_target_pairs={{0,32},{32,0},{64,96},{96,64},{128,160},{160,128},{192,224},{224,1... | collective-permute-start | bytes 221192 | tf_op jit(solution)/shard_map/ppermute | solution.py:33
  84.2 11.9 %collective-permute-start.21 = (f32[80,384]{1,0:T(8,128)S(1)}, f32[80,384]{1,0:T(8,128)S(1)}, u32[]{:S(2)}, u32[]{:S(2)}) collective-permute-start(f32[80,384]{1,0:T(8,128)S(1)} %get-tuple-element.90), channel_id=1, source_target_pairs={{0,128},{32,160},{64,192},{96,224},{128,0},{160,32},{192,64},{224,... | collective-permute-start | bytes 368648 | tf_op jit(solution)/shard_map/ppermute | solution.py:29
  91.6 8.4 %collective-permute-start.22 = (f32[80,384]{1,0:T(8,128)S(1)}, f32[80,384]{1,0:T(8,128)S(1)}, u32[]{:S(2)}, u32[]{:S(2)}) collective-permute-start(f32[80,384]{1,0:T(8,128)S(1)} %get-tuple-element.91), channel_id=1, source_target_pairs={{0,64},{32,96},{64,128},{96,160},{128,192},{160,224},{192,0},{224,... | collective-permute-start | bytes 368648 | tf_op jit(solution)/shard_map/ppermute | solution.py:29
  92.8 8.4 %collective-permute-start.23 = (f32[80,384]{1,0:T(8,128)S(1)}, f32[80,384]{1,0:T(8,128)S(1)}, u32[]{:S(2)}, u32[]{:S(2)}) collective-permute-start(f32[80,384]{1,0:T(8,128)S(1)} %get-tuple-element.89), channel_id=1, source_target_pairs={{0,192},{32,224},{64,0},{96,32},{128,64},{160,96},{192,128},{224,1... | collective-permute-start | bytes 368648 | tf_op jit(solution)/shard_map/ppermute | solution.py:29
  101.3 7.4 %collective-permute-start.28 = (f32[32,384]{1,0:T(8,128)S(1)}, f32[32,384]{1,0:T(8,128)S(1)}, u32[]{:S(2)}, u32[]{:S(2)}) collective-permute-start(f32[32,384]{1,0:T(8,128)S(1)} %slice.23), channel_id=1, source_target_pairs={{0,32},{32,0},{64,96},{96,64},{128,160},{160,128},{192,224},{224,1... | collective-permute-start | bytes 147464 | tf_op jit(solution)/shard_map/ppermute | solution.py:33
  102.2 10.8 %collective-permute-start.24 = (f32[2,48,384]{2,1,0:T(8,128)S(1)}, f32[2,48,384]{2,1,0:T(8,128)S(1)}, u32[]{:S(2)}, u32[]{:S(2)}) collective-permute-start(f32[2,48,384]{2,1,0:T(8,128)S(1)} %pad_maximum_fusion.4), channel_id=1, source_target_pairs={{0,6},{8,14},{2,0},{10,8},{4,2},{12,10},{6,4},{14,12},{1,7},{9,15}... | collective-permute-start | bytes 442376 | tf_op jit(solution)/shard_map/ppermute | solution.py:21
  104.5 9.7 %collective-permute-start.25 = (f32[2,48,384]{2,1,0:T(8,128)S(1)}, f32[2,48,384]{2,1,0:T(8,128)S(1)}, u32[]{:S(2)}, u32[]{:S(2)}) collective-permute-start(f32[2,48,384]{2,1,0:T(8,128)S(1)} %pad_maximum_fusion.4), channel_id=1, source_target_pairs={{0,4},{8,12},{2,6},{10,14},{4,0},{12,8},{6,2},{14,10},{1,5},{9,13}... | collective-permute-start | bytes 442376 | tf_op jit(solution)/shard_map/ppermute | solution.py:21
  106.2 8.1 %collective-permute-start.26 = (f32[2,48,384]{2,1,0:T(8,128)S(1)}, f32[2,48,384]{2,1,0:T(8,128)S(1)}, u32[]{:S(2)}, u32[]{:S(2)}) collective-permute-start(f32[2,48,384]{2,1,0:T(8,128)S(1)} %pad_maximum_fusion.4), channel_id=1, source_target_pairs={{0,2},{8,10},{2,4},{10,12},{4,6},{12,14},{6,0},{14,8},{1,3},{9,11}... | collective-permute-start | bytes 442376 | tf_op jit(solution)/shard_map/ppermute | solution.py:21
  108.7 7.0 %collective-permute-start.29 = (f32[64,384]{1,0:T(8,128)S(1)}, f32[64,384]{1,0:T(8,128)S(1)}, u32[]{:S(2)}, u32[]{:S(2)}) collective-permute-start(f32[64,384]{1,0:T(8,128)S(1)} %fusion.3), channel_id=1, source_target_pairs={{0,192},{32,224},{64,0},{96,32},{128,64},{160,96},{192,128},{224,1... | collective-permute-start | bytes 294920 | tf_op jit(solution)/shard_map/ppermute | solution.py:29
  111.8 9.9 %collective-permute-start.30 = (f32[64,384]{1,0:T(8,128)S(1)}, f32[64,384]{1,0:T(8,128)S(1)}, u32[]{:S(2)}, u32[]{:S(2)}) collective-permute-start(f32[64,384]{1,0:T(8,128)S(1)} %fusion.3), channel_id=1, source_target_pairs={{0,128},{32,160},{64,192},{96,224},{128,0},{160,32},{192,64},{224,... | collective-permute-start | bytes 294920 | tf_op jit(solution)/shard_map/ppermute | solution.py:29
  113.1 9.2 %collective-permute-start.31 = (f32[64,384]{1,0:T(8,128)S(1)}, f32[64,384]{1,0:T(8,128)S(1)}, u32[]{:S(2)}, u32[]{:S(2)}) collective-permute-start(f32[64,384]{1,0:T(8,128)S(1)} %fusion.3), channel_id=1, source_target_pairs={{0,64},{32,96},{64,128},{96,160},{128,192},{160,224},{192,0},{224,... | collective-permute-start | bytes 294920 | tf_op jit(solution)/shard_map/ppermute | solution.py:29
  114.4 8.7 %collective-permute-start.27 = (f32[2,192,384]{2,1,0:T(8,128)S(1)}, f32[2,192,384]{2,1,0:T(8,128)S(1)}, u32[]{:S(2)}, u32[]{:S(2)}) collective-permute-start(f32[2,192,384]{2,1,0:T(8,128)S(1)} %constant_dynamic-slice_fusion.1.mine), channel_id=1, source_target_pairs={{0,8},{8,0},{2,10},{10,2},{4,12},{12,4},{6,14},{14,6},{1,9},{9,1},... | collective-permute-start | bytes 1769480 | tf_op jit(solution)/shard_map/ppermute | solution.py:21

commit v2 on v1

--- a/solution.py
+++ b/solution.py
@@ -167,6 +167,17 @@
     )(info, *panel, *halves)
 
 
+def join_kernel(p_up, up, p_down, down, for_up, for_down):
+    for_up[...] = p_up[...] + up[...]
+    for_down[...] = p_down[...] + down[...]
+
+
+def join(*arrays):
+    rows, width = arrays[0].shape
+    out_shape = [jax.ShapeDtypeStruct((rows, width), jnp.float32)] * 2
+    return local(join_kernel, [VMEM] * 4, out_shape, 2 * rows * width, 24 * rows * width)(*arrays)
+
+
 def turn_kernel(own, other, own_high, own_low, other_high, other_low):
     own_high[...], own_low[...] = split(own[...].T)
     other_high[...], other_low[...] = split(other[...].T)
@@ -289,7 +300,8 @@
     p11, p30 = next_dot(straight, halves, panel, rows, 2)
     up1, down0 = shift(p11, dy=1), shift(p30, dy=-1)
     p10, p31, p00, p01 = next_dot(joined, halves, panel, rows, 4)
-    up0, down1 = shift(p10 + up, dy=1), shift(p31 + down, dy=-1)
+    for_up, for_down = join(p10, up, p31, down)
+    up0, down1 = shift(for_up, dy=1), shift(for_down, dy=-1)
     kept, sent, sum_own, sum_other = correction(tail, p00, p01, up0, down0, up1, down1, *turned(own, flip_x(own)))
 
     pair, four = z % 2, z // 2

time: 124 us -> 124 us (level)
  waiting for transfers between devices: 41.4 us -> 38.5 us
  starting transfers between devices: 59.4 us -> 62 us
    ppermute x6, starting transfers between devices: 17 us -> 18.7 us  [along_pole(): return lax.ppermute(value, 'pole', [(z, (z + step) % 8) for z in range(8)])]
    ppermute x6, waiting for transfers between devices: 13.1 us -> 11.6 us  [along_pole(): return lax.ppermute(value, 'pole', [(z, (z + step) % 8) for z in range(8)])]
    ppermute x19, waiting for transfers between devices: 21.6 us -> 20.1 us  [shift(): return lax.ppermute(value, PLANE, pairs)]
    ppermute x19, starting transfers between devices: 29.6 us -> 30.9 us  [shift(): return lax.ppermute(value, PLANE, pairs)]
  transfers between devices with their start and end apart: 32 -> 32, of which waited for: 19 -> 17; matrix products, arithmetic and copies ran while one was open for 3% -> 3% of each run, Pallas kernels for 8% -> 8%
where the time goes in v2:
time: 124 us
  starting transfers between devices  62 us (50%)
  waiting for transfers between devices  38.5 us (31%)
  Pallas kernels  14.8 us (12%)
  local copies, waits for them, and re-layouts  5.99 us (5%)
  between operations  1.7 us (1%)
    ppermute x19, starting transfers between devices, shift(): return lax.ppermute(value, PLANE, pairs)  30.9 us
    ppermute x19, waiting for transfers between devices, shift(): return lax.ppermute(value, PLANE, pairs)  20.1 us
    ppermute x6, starting transfers between devices, along_pole(): return lax.ppermute(value, 'pole', [(z, (z + step) % 8) for z in range(8)])  18.7 us
    ppermute x6, waiting for transfers between devices, along_pole(): return lax.ppermute(value, 'pole', [(z, (z + step) % 8) for z in range(8)])  11.6 us
    ppermute x2, starting transfers between devices, panel_slot(): return lax.ppermute(value, PLANE, pairs)  7.71 us
    pallas_call x2, Pallas kernels, next_dot(): local(next_kernel, [SMEM] + [VMEM] * 4, out_shape, count * 6 * rows * dep...  6.38 us
    ppermute x3, starting transfers between devices, pole_pair(): return lax.ppermute(value, 'pole', [(z, z ^ 1) for z in range(8)])  4.68 us
    ppermute x2, waiting for transfers between devices, panel_slot(): return lax.ppermute(value, PLANE, pairs)  3.67 us
  transfers between devices with their start and end apart: 32, of which 17 were waited for; matrix products, arithmetic and copies ran while one was open for 3% of the time, Pallas kernels for 8%

profile of v2, /device:TPU:8, one launch (start us, length us, event | category | flops | bytes accessed | tf_op | source)
XLA Modules:
  0.0 124.0 jit_solution(8417525749840149653)
XLA Ops:
  0.6 2.1 %collective-permute-start = (f32[256,384]{1,0:T(8,128)}, f32[256,384]{1,0:T(8,128)S(1)}, u32[]{:S(2)}, u32[]{:S(2)}) collective-permute-start(f32[256,384]{1,0:T(8,128)} %bitcast.36), channel_id=1, source_target_pairs={{0,0},{2,8},{8,2},{10,10},{16,4},{18,12},{24,6},{26,14},{4,1},{6,9... | collective-permute-start | bytes 1179656 | tf_op jit(solution)/shard_map/ppermute | solution.py:42
  2.7 5.7 %collective-permute-start.1 = (f32[256,384]{1,0:T(8,128)}, f32[256,384]{1,0:T(8,128)S(1)}, u32[]{:S(2)}, u32[]{:S(2)}) collective-permute-start(f32[256,384]{1,0:T(8,128)} %bitcast.37), channel_id=1, source_target_pairs={{1,0},{3,8},{9,2},{11,10},{17,4},{19,12},{25,6},{27,14},{5,1},{7,9... | collective-permute-start | bytes 1179656 | tf_op jit(solution)/shard_map/ppermute | solution.py:42
  8.8 1.3 %gather_fusion = s32[6]{0:T(128)S(1)} fusion(s32[32]{0:T(128)} %param.9, s32[1024]{0:T(1024)S(1)} %pad_clamp_fusion), kind=kCustom, calls=%fused_computation | custom fusion | bytes 72 | tf_op jit(solution)/shard_map/jit(_take)/gather | solution.py:278
  10.4 3.4 %copy-done.1 = f32[1,2048,1024]{2,1,0:T(8,128)S(1)} copy-done((f32[1,2048,1024]{2,1,0:T(8,128)S(1)}, f32[1,2048,1024]{2,1,0:T(8,128)}, u32[]{:S(2)}) %copy-start.1) | copy-done | bytes 8388632
  13.8 1.1 shard_map.84
  15.1 3.7 %collective-permute-done.s0 = f32[256,384]{1,0:T(8,128)S(1)} collective-permute-done((f32[256,384]{1,0:T(8,128)}, f32[256,384]{1,0:T(8,128)S(1)}, u32[]{:S(2)}, u32[]{:S(2)}) %collective-permute-start) | collective-permute-done | bytes 393248 | tf_op jit(solution)/shard_map/ppermute | solution.py:42
  19.3 1.7 %shard_map.85 = (f32[256,384]{1,0:T(8,128)S(1)}, f32[256,384]{1,0:T(8,128)S(1)}, bf16[512,384]{1,0:T(8,128)(2,1)S(1)}, bf16[512,384]{1,0:T(8,128)(2,1)S(1)}) custom-call(s32[7]{0:T(128)S(1)} %concatenate.90.info, f32[256,384]{1,0:T(8,128)S(1)} %collective-permute-done.s0, f32[256,384]{1,0:T(8,128)S(1)} %collective-permute-done.1.s1, ...), custom_call_target="tpu_custom_call" | custom-call | flops 603979776 | bytes 3407872 | tf_op jit(solution)/shard_map/pallas_call | solution.py:138
  21.1 1.9 %shard_map.86 = (f32[256,384]{1,0:T(8,128)S(1)}, f32[256,384]{1,0:T(8,128)S(1)}, bf16[1024,384]{1,0:T(8,128)(2,1)S(1)}, bf16[1024,384]{1,0:T(8,128)(2,1)S(1)}) custom-call(s32[7]{0:T(128)S(1)} %concatenate.91.info, f32[256,384]{1,0:T(8,128)S(1)} %collective-permute-done.2.t0, f32[256,384]{1,0:T(8,128)S(1)} %collective-permute-done.3.t1, ...), custom_call_target="tpu_custom_call" | custom-call | flops 603979776 | bytes 4980736 | tf_op jit(solution)/shard_map/pallas_call | solution.py:148
  23.0 9.3 %collective-permute-start.4 = (f32[256,384]{1,0:T(8,128)S(1)}, f32[256,384]{1,0:T(8,128)S(1)}, u32[]{:S(2)}, u32[]{:S(2)}) collective-permute-start(f32[256,384]{1,0:T(8,128)S(1)} %get-tuple-element.63), channel_id=1, source_target_pairs={{0,2},{8,10},{2,4},{10,12},{4,6},{12,14},{6,0},{14,8},{1,3},{9,11}... | collective-permute-start | bytes 1179656 | tf_op jit(solution)/shard_map/ppermute | solution.py:21
  32.3 2.4 %shard_map.89 = (f32[256,384]{1,0:T(8,128)S(1)}, f32[256,384]{1,0:T(8,128)S(1)}) custom-call(s32[2]{0:T(128)S(1)} %pad_add_fusion.info, bf16[1024,384]{1,0:T(8,128)(2,1)S(1)} %get-tuple-element.58.high, bf16[1024,384]{1,0:T(8,128)(2,1)S(1)} %get-tuple-element.59.low, bf16[2048,1024]{1,0:T(8,128)(2,1)S(1)} %get-tuple-element.52.a_high, ...), custom_call_target="tpu_custom_call" | custom-call | flops 1207959552 | bytes 2883584 | tf_op jit(solution)/shard_map/pallas_call | solution.py:161
  34.7 2.8 %collective-permute-start.7 = (f32[256,384]{1,0:T(8,128)S(1)}, f32[256,384]{1,0:T(8,128)S(1)}, u32[]{:S(2)}, u32[]{:S(2)}) collective-permute-start(f32[256,384]{1,0:T(8,128)S(1)} %get-tuple-element.68), channel_id=1, source_target_pairs={{0,6},{8,14},{2,0},{10,8},{4,2},{12,10},{6,4},{14,12},{1,7},{9,15}... | collective-permute-start | bytes 1179656 | tf_op jit(solution)/shard_map/ppermute | solution.py:21
  37.5 4.0 %shard_map.87 = (f32[256,384]{1,0:T(8,128)S(1)}, f32[256,384]{1,0:T(8,128)S(1)}, f32[256,384]{1,0:T(8,128)S(1)}, f32[256,384]{1,0:T(8,128)S(1)}) custom-call(s32[4]{0:T(128)S(1)} %get-tuple-element.47.info, bf16[1024,384]{1,0:T(8,128)(2,1)S(1)} %get-tuple-element.58.high, bf16[1024,384]{1,0:T(8,128)(2,1)S(1)} %get-tuple-element.59.low, ...), custom_call_target="tpu_custom_call" | custom-call | flops 2415919104 | bytes 5767168 | tf_op jit(solution)/shard_map/pallas_call | solution.py:161
  41.8 2.5 %collective-permute-done.5.down = f32[256,384]{1,0:T(8,128)S(1)} collective-permute-done((f32[256,384]{1,0:T(8,128)S(1)}, f32[256,384]{1,0:T(8,128)S(1)}, u32[]{:S(2)}, u32[]{:S(2)}) %collective-permute-start.5) | collective-permute-done | bytes 393248 | tf_op jit(solution)/shard_map/ppermute | solution.py:21
  44.4 1.2 collective-permute-start.6
  45.6 0.9 collective-permute-start.9
  46.8 5.9 %collective-permute-done.7.down0 = f32[256,384]{1,0:T(8,128)S(1)} collective-permute-done((f32[256,384]{1,0:T(8,128)S(1)}, f32[256,384]{1,0:T(8,128)S(1)}, u32[]{:S(2)}, u32[]{:S(2)}) %collective-permute-start.7) | collective-permute-done | bytes 393248 | tf_op jit(solution)/shard_map/ppermute | solution.py:21
  52.8 5.1 %collective-permute-done.6.up0 = f32[256,384]{1,0:T(8,128)S(1)} collective-permute-done((f32[256,384]{1,0:T(8,128)S(1)}, f32[256,384]{1,0:T(8,128)S(1)}, u32[]{:S(2)}, u32[]{:S(2)}) %collective-permute-start.6) | collective-permute-done | bytes 393248 | tf_op jit(solution)/shard_map/ppermute | solution.py:21
  57.8 2.2 %collective-permute-done.9.down1 = f32[256,384]{1,0:T(8,128)S(1)} collective-permute-done((f32[256,384]{1,0:T(8,128)S(1)}, f32[256,384]{1,0:T(8,128)S(1)}, u32[]{:S(2)}, u32[]{:S(2)}) %collective-permute-start.9) | collective-permute-done | bytes 393248 | tf_op jit(solution)/shard_map/ppermute | solution.py:21
  60.0 1.5 %shard_map.91 = (f32[192,384]{1,0:T(8,128)S(1)}, f32[192,384]{1,0:T(8,128)S(1)}, f32[256,384]{1,0:T(8,128)S(1)}, f32[256,384]{1,0:T(8,128)S(1)}) custom-call(s32[4]{0:T(128)S(1)} %get-tuple-element.46.info, f32[256,384]{1,0:T(8,128)S(1)} %get-tuple-element.60.p0, f32[256,384]{1,0:T(8,128)S(1)} %get-tuple-element.61.p1, ...), custom_call_target="tpu_custom_call" | custom-call | flops 452984832 | bytes 4718592 | tf_op jit(solution)/shard_map/pallas_call | solution.py:210
  61.7 1.4 %collective-permute-done.12 = f32[192,384]{1,0:T(8,128)S(1)} collective-permute-done((f32[192,384]{1,0:T(8,128)S(1)}, f32[192,384]{1,0:T(8,128)S(1)}, u32[]{:S(2)}, u32[]{:S(2)}) %collective-permute-start.12) | collective-permute-done | bytes 294944 | tf_op jit(solution)/shard_map/ppermute | solution.py:21
  63.3 2.2 %collective-permute-start.13 = (f32[48,384]{1,0:T(8,128)S(1)}, f32[48,384]{1,0:T(8,128)S(1)}, u32[]{:S(2)}, u32[]{:S(2)}) collective-permute-start(f32[48,384]{1,0:T(8,128)S(1)} %get-tuple-element.86), channel_id=1, source_target_pairs={{0,4},{8,12},{2,6},{10,14},{4,0},{12,8},{6,2},{14,10},{1,5},{9,13}... | collective-permute-start | bytes 221192 | tf_op jit(solution)/shard_map/ppermute | solution.py:21
  65.4 2.0 %collective-permute-start.15 = (f32[48,384]{1,0:T(8,128)S(1)}, f32[48,384]{1,0:T(8,128)S(1)}, u32[]{:S(2)}, u32[]{:S(2)}) collective-permute-start(f32[48,384]{1,0:T(8,128)S(1)} %get-tuple-element.87), channel_id=1, source_target_pairs={{0,6},{8,14},{2,0},{10,8},{4,2},{12,10},{6,4},{14,12},{1,7},{9,15}... | collective-permute-start | bytes 221192 | tf_op jit(solution)/shard_map/ppermute | solution.py:21
  68.1 1.3 %collective-permute-done.13 = f32[48,384]{1,0:T(8,128)S(1)} collective-permute-done((f32[48,384]{1,0:T(8,128)S(1)}, f32[48,384]{1,0:T(8,128)S(1)}, u32[]{:S(2)}, u32[]{:S(2)}) %collective-permute-start.13) | collective-permute-done | bytes 73760 | tf_op jit(solution)/shard_map/ppermute | solution.py:21
  69.4 0.9 collective-permute-done.14
  70.8 2.4 %collective-permute-start.16 = (f32[48,384]{1,0:T(8,128)S(1)}, f32[48,384]{1,0:T(8,128)S(1)}, u32[]{:S(2)}, u32[]{:S(2)}) collective-permute-start(f32[48,384]{1,0:T(8,128)S(1)} %add_add_fusion.1), channel_id=1, source_target_pairs={{0,16},{8,24},{2,18},{10,26},{4,20},{12,28},{6,22},{14,30},{1,17},... | collective-permute-start | bytes 221192 | tf_op jit(solution)/shard_map/ppermute | solution.py:21
  73.1 0.8 collective-permute-start.17
  74.0 2.4 %collective-permute-start.18 = (f32[48,384]{1,0:T(8,128)S(1)}, f32[48,384]{1,0:T(8,128)S(1)}, u32[]{:S(2)}, u32[]{:S(2)}) collective-permute-start(f32[48,384]{1,0:T(8,128)S(1)} %add_add_fusion.1), channel_id=1, source_target_pairs={{0,17},{8,25},{2,19},{10,27},{4,21},{12,29},{6,23},{14,31},{1,0},{... | collective-permute-start | bytes 221192 | tf_op jit(solution)/shard_map/ppermute | solution.py:21
  76.4 0.8 shard_map.92
  77.2 2.0 %collective-permute-start.19 = (f32[128,384]{1,0:T(8,128)S(1)}, f32[128,384]{1,0:T(8,128)S(1)}, u32[]{:S(2)}, u32[]{:S(2)}) collective-permute-start(f32[128,384]{1,0:T(8,128)S(1)} %constant_dynamic-slice_fusion.6), channel_id=1, source_target_pairs={{0,32},{32,0},{64,96},{96,64},{128,160},{160,128},{192,224},{224,1... | collective-permute-start | bytes 589832 | tf_op jit(solution)/shard_map/ppermute | solution.py:33
  79.2 1.7 %collective-permute-start.20 = (f32[48,384]{1,0:T(8,128)S(1)}, f32[48,384]{1,0:T(8,128)S(1)}, u32[]{:S(2)}, u32[]{:S(2)}) collective-permute-start(f32[48,384]{1,0:T(8,128)S(1)} %get-tuple-element.84), channel_id=1, source_target_pairs={{0,32},{32,0},{64,96},{96,64},{128,160},{160,128},{192,224},{224,1... | collective-permute-start | bytes 221192 | tf_op jit(solution)/shard_map/ppermute | solution.py:33
  80.9 3.1 %collective-permute-done.20 = f32[48,384]{1,0:T(8,128)S(1)} collective-permute-done((f32[48,384]{1,0:T(8,128)S(1)}, f32[48,384]{1,0:T(8,128)S(1)}, u32[]{:S(2)}, u32[]{:S(2)}) %collective-permute-start.20) | collective-permute-done | bytes 73760 | tf_op jit(solution)/shard_map/ppermute | solution.py:33
  84.2 7.5 %collective-permute-start.21 = (f32[80,384]{1,0:T(8,128)S(1)}, f32[80,384]{1,0:T(8,128)S(1)}, u32[]{:S(2)}, u32[]{:S(2)}) collective-permute-start(f32[80,384]{1,0:T(8,128)S(1)} %get-tuple-element.94), channel_id=1, source_target_pairs={{0,128},{32,160},{64,192},{96,224},{128,0},{160,32},{192,64},{224,... | collective-permute-start | bytes 368648 | tf_op jit(solution)/shard_map/ppermute | solution.py:29
  91.7 1.1 collective-permute-start.22
  92.8 3.1 %collective-permute-start.23 = (f32[80,384]{1,0:T(8,128)S(1)}, f32[80,384]{1,0:T(8,128)S(1)}, u32[]{:S(2)}, u32[]{:S(2)}) collective-permute-start(f32[80,384]{1,0:T(8,128)S(1)} %get-tuple-element.93), channel_id=1, source_target_pairs={{0,192},{32,224},{64,0},{96,32},{128,64},{160,96},{192,128},{224,1... | collective-permute-start | bytes 368648 | tf_op jit(solution)/shard_map/ppermute | solution.py:29
  95.9 0.6 collective-permute-done.21
  96.4 4.0 %collective-permute-done.22 = f32[80,384]{1,0:T(8,128)S(1)} collective-permute-done((f32[80,384]{1,0:T(8,128)S(1)}, f32[80,384]{1,0:T(8,128)S(1)}, u32[]{:S(2)}, u32[]{:S(2)}) %collective-permute-start.22) | collective-permute-done | bytes 122912 | tf_op jit(solution)/shard_map/ppermute | solution.py:29
  100.4 0.8 collective-permute-done.23
  101.2 1.0 collective-permute-start.28
  102.2 1.4 %collective-permute-start.24 = (f32[2,48,384]{2,1,0:T(8,128)S(1)}, f32[2,48,384]{2,1,0:T(8,128)S(1)}, u32[]{:S(2)}, u32[]{:S(2)}) collective-permute-start(f32[2,48,384]{2,1,0:T(8,128)S(1)} %pad_maximum_fusion.4), channel_id=1, source_target_pairs={{0,6},{8,14},{2,0},{10,8},{4,2},{12,10},{6,4},{14,12},{1,7},{9,15}... | collective-permute-start | bytes 442376 | tf_op jit(solution)/shard_map/ppermute | solution.py:21
  103.7 2.1 %collective-permute-start.25 = (f32[2,48,384]{2,1,0:T(8,128)S(1)}, f32[2,48,384]{2,1,0:T(8,128)S(1)}, u32[]{:S(2)}, u32[]{:S(2)}) collective-permute-start(f32[2,48,384]{2,1,0:T(8,128)S(1)} %pad_maximum_fusion.4), channel_id=1, source_target_pairs={{0,4},{8,12},{2,6},{10,14},{4,0},{12,8},{6,2},{14,10},{1,5},{9,13}... | collective-permute-start | bytes 442376 | tf_op jit(solution)/shard_map/ppermute | solution.py:21
  105.8 2.5 %collective-permute-start.26 = (f32[2,48,384]{2,1,0:T(8,128)S(1)}, f32[2,48,384]{2,1,0:T(8,128)S(1)}, u32[]{:S(2)}, u32[]{:S(2)}) collective-permute-start(f32[2,48,384]{2,1,0:T(8,128)S(1)} %pad_maximum_fusion.4), channel_id=1, source_target_pairs={{0,2},{8,10},{2,4},{10,12},{4,6},{12,14},{6,0},{14,8},{1,3},{9,11}... | collective-permute-start | bytes 442376 | tf_op jit(solution)/shard_map/ppermute | solution.py:21
  108.3 3.8 %collective-permute-start.29 = (f32[64,384]{1,0:T(8,128)S(1)}, f32[64,384]{1,0:T(8,128)S(1)}, u32[]{:S(2)}, u32[]{:S(2)}) collective-permute-start(f32[64,384]{1,0:T(8,128)S(1)} %fusion.3), channel_id=1, source_target_pairs={{0,192},{32,224},{64,0},{96,32},{128,64},{160,96},{192,128},{224,1... | collective-permute-start | bytes 294920 | tf_op jit(solution)/shard_map/ppermute | solution.py:29
  112.2 1.7 %collective-permute-start.30 = (f32[64,384]{1,0:T(8,128)S(1)}, f32[64,384]{1,0:T(8,128)S(1)}, u32[]{:S(2)}, u32[]{:S(2)}) collective-permute-start(f32[64,384]{1,0:T(8,128)S(1)} %fusion.3), channel_id=1, source_target_pairs={{0,128},{32,160},{64,192},{96,224},{128,0},{160,32},{192,64},{224,... | collective-permute-start | bytes 294920 | tf_op jit(solution)/shard_map/ppermute | solution.py:29
  113.9 1.5 %collective-permute-start.31 = (f32[64,384]{1,0:T(8,128)S(1)}, f32[64,384]{1,0:T(8,128)S(1)}, u32[]{:S(2)}, u32[]{:S(2)}) collective-permute-start(f32[64,384]{1,0:T(8,128)S(1)} %fusion.3), channel_id=1, source_target_pairs={{0,64},{32,96},{64,128},{96,160},{128,192},{160,224},{192,0},{224,... | collective-permute-start | bytes 294920 | tf_op jit(solution)/shard_map/ppermute | solution.py:29
  115.7 3.5 %collective-permute-done.29 = f32[64,384]{1,0:T(8,128)S(1)} collective-permute-done((f32[64,384]{1,0:T(8,128)S(1)}, f32[64,384]{1,0:T(8,128)S(1)}, u32[]{:S(2)}, u32[]{:S(2)}) %collective-permute-start.29) | collective-permute-done | bytes 98336 | tf_op jit(solution)/shard_map/ppermute | solution.py:29
  119.2 2.8 %collective-permute-done.30 = f32[64,384]{1,0:T(8,128)S(1)} collective-permute-done((f32[64,384]{1,0:T(8,128)S(1)}, f32[64,384]{1,0:T(8,128)S(1)}, u32[]{:S(2)}, u32[]{:S(2)}) %collective-permute-start.30) | collective-permute-done | bytes 98336 | tf_op jit(solution)/shard_map/ppermute | solution.py:29
  122.1 0.8 constant_dynamic-slice_fusion
  122.9 1.1 shard_map.93
  (76 shorter events, 3.3 us)
Async XLA Ops:
  0.6 14.5 %copy-start = (f32[1,384,384]{2,1,0:T(8,128)S(1)}, f32[1,384,384]{2,1,0:T(8,128)}, u32[]{:S(2)}) copy-start(f32[1,384,384]{2,1,0:T(8,128)} %param.7) | copy-start | bytes 1769476
  0.6 18.1 %collective-permute-start = (f32[256,384]{1,0:T(8,128)}, f32[256,384]{1,0:T(8,128)S(1)}, u32[]{:S(2)}, u32[]{:S(2)}) collective-permute-start(f32[256,384]{1,0:T(8,128)} %bitcast.36), channel_id=1, source_target_pairs={{0,0},{2,8},{8,2},{10,10},{16,4},{18,12},{24,6},{26,14},{4,1},{6,9... | collective-permute-start | bytes 1179656 | tf_op jit(solution)/shard_map/ppermute | solution.py:42
  2.7 16.1 %collective-permute-start.1 = (f32[256,384]{1,0:T(8,128)}, f32[256,384]{1,0:T(8,128)S(1)}, u32[]{:S(2)}, u32[]{:S(2)}) collective-permute-start(f32[256,384]{1,0:T(8,128)} %bitcast.37), channel_id=1, source_target_pairs={{1,0},{3,8},{9,2},{11,10},{17,4},{19,12},{25,6},{27,14},{5,1},{7,9... | collective-permute-start | bytes 1179656 | tf_op jit(solution)/shard_map/ppermute | solution.py:42
  10.4 3.4 %copy-start.1 = (f32[1,2048,1024]{2,1,0:T(8,128)S(1)}, f32[1,2048,1024]{2,1,0:T(8,128)}, u32[]{:S(2)}) copy-start(f32[1,2048,1024]{2,1,0:T(8,128)} %param.5) | copy-start | bytes 25165828
  18.8 2.2 %collective-permute-start.2 = (f32[256,384]{1,0:T(8,128)S(1)}, f32[256,384]{1,0:T(8,128)S(1)}, u32[]{:S(2)}, u32[]{:S(2)}) collective-permute-start(f32[256,384]{1,0:T(8,128)S(1)} %collective-permute-done.s0), channel_id=1, source_target_pairs={{0,8},{8,0},{2,10},{10,2},{4,12},{12,4},{6,14},{14,6},{1,9},{9,1},... | collective-permute-start | bytes 1179656 | tf_op jit(solution)/shard_map/ppermute | solution.py:21
  18.8 2.3 %collective-permute-start.3 = (f32[256,384]{1,0:T(8,128)S(1)}, f32[256,384]{1,0:T(8,128)S(1)}, u32[]{:S(2)}, u32[]{:S(2)}) collective-permute-start(f32[256,384]{1,0:T(8,128)S(1)} %collective-permute-done.1.s1), channel_id=1, source_target_pairs={{0,8},{8,0},{2,10},{10,2},{4,12},{12,4},{6,14},{14,6},{1,9},{9,1},... | collective-permute-start | bytes 1179656 | tf_op jit(solution)/shard_map/ppermute | solution.py:21
  21.1 11.3 %copy-start.2 = (f32[1,256,384]{2,1,0:T(8,128)S(1)}, f32[1,256,384]{2,1,0:T(8,128)}, u32[]{:S(2)}) copy-start(f32[1,256,384]{2,1,0:T(8,128)} %param.6) | copy-start | bytes 1179652
  23.0 18.8 %collective-permute-start.4 = (f32[256,384]{1,0:T(8,128)S(1)}, f32[256,384]{1,0:T(8,128)S(1)}, u32[]{:S(2)}, u32[]{:S(2)}) collective-permute-start(f32[256,384]{1,0:T(8,128)S(1)} %get-tuple-element.63), channel_id=1, source_target_pairs={{0,2},{8,10},{2,4},{10,12},{4,6},{12,14},{6,0},{14,8},{1,3},{9,11}... | collective-permute-start | bytes 1179656 | tf_op jit(solution)/shard_map/ppermute | solution.py:21
  32.3 12.0 %collective-permute-start.5 = (f32[256,384]{1,0:T(8,128)S(1)}, f32[256,384]{1,0:T(8,128)S(1)}, u32[]{:S(2)}, u32[]{:S(2)}) collective-permute-start(f32[256,384]{1,0:T(8,128)S(1)} %get-tuple-element.65), channel_id=1, source_target_pairs={{0,6},{8,14},{2,0},{10,8},{4,2},{12,10},{6,4},{14,12},{1,7},{9,15}... | collective-permute-start | bytes 1179656 | tf_op jit(solution)/shard_map/ppermute | solution.py:21
  32.3 14.2 %collective-permute-start.10 = (f32[256,384]{1,0:T(8,128)S(1)}, f32[256,384]{1,0:T(8,128)S(1)}, u32[]{:S(2)}, u32[]{:S(2)}) collective-permute-start(f32[256,384]{1,0:T(8,128)S(1)} %bitcast.38), channel_id=1, source_target_pairs={{0,1},{8,9},{2,3},{10,11},{4,5},{12,13},{6,7},{14,15},{1,0},{9,8},... | collective-permute-start | bytes 1179656 | tf_op jit(solution)/shard_map/ppermute | solution.py:25
  34.7 18.1 %collective-permute-start.7 = (f32[256,384]{1,0:T(8,128)S(1)}, f32[256,384]{1,0:T(8,128)S(1)}, u32[]{:S(2)}, u32[]{:S(2)}) collective-permute-start(f32[256,384]{1,0:T(8,128)S(1)} %get-tuple-element.68), channel_id=1, source_target_pairs={{0,6},{8,14},{2,0},{10,8},{4,2},{12,10},{6,4},{14,12},{1,7},{9,15}... | collective-permute-start | bytes 1179656 | tf_op jit(solution)/shard_map/ppermute | solution.py:21
  37.5 15.2 %collective-permute-start.8 = (f32[256,384]{1,0:T(8,128)S(1)}, f32[256,384]{1,0:T(8,128)S(1)}, u32[]{:S(2)}, u32[]{:S(2)}) collective-permute-start(f32[256,384]{1,0:T(8,128)S(1)} %get-tuple-element.69), channel_id=1, source_target_pairs={{0,2},{8,10},{2,4},{10,12},{4,6},{12,14},{6,0},{14,8},{1,3},{9,11}... | collective-permute-start | bytes 1179656 | tf_op jit(solution)/shard_map/ppermute | solution.py:21
  44.4 13.4 %collective-permute-start.6 = (f32[256,384]{1,0:T(8,128)S(1)}, f32[256,384]{1,0:T(8,128)S(1)}, u32[]{:S(2)}, u32[]{:S(2)}) collective-permute-start(f32[256,384]{1,0:T(8,128)S(1)} %get-tuple-element.66), channel_id=1, source_target_pairs={{0,2},{8,10},{2,4},{10,12},{4,6},{12,14},{6,0},{14,8},{1,3},{9,11}... | collective-permute-start | bytes 1179656 | tf_op jit(solution)/shard_map/ppermute | solution.py:21
  45.6 14.5 %collective-permute-start.9 = (f32[256,384]{1,0:T(8,128)S(1)}, f32[256,384]{1,0:T(8,128)S(1)}, u32[]{:S(2)}, u32[]{:S(2)}) collective-permute-start(f32[256,384]{1,0:T(8,128)S(1)} %get-tuple-element.70), channel_id=1, source_target_pairs={{0,6},{8,14},{2,0},{10,8},{4,2},{12,10},{6,4},{14,12},{1,7},{9,15}... | collective-permute-start | bytes 1179656 | tf_op jit(solution)/shard_map/ppermute | solution.py:21
  61.5 1.7 %collective-permute-start.12 = (f32[192,384]{1,0:T(8,128)S(1)}, f32[192,384]{1,0:T(8,128)S(1)}, u32[]{:S(2)}, u32[]{:S(2)}) collective-permute-start(f32[192,384]{1,0:T(8,128)S(1)} %get-tuple-element.80), channel_id=1, source_target_pairs={{0,8},{8,0},{2,10},{10,2},{4,12},{12,4},{6,14},{14,6},{1,9},{9,1},... | collective-permute-start | bytes 884744 | tf_op jit(solution)/shard_map/ppermute | solution.py:21
  61.6 14.7 %collective-permute-start.11 = (f32[256,384]{1,0:T(8,128)S(1)}, f32[256,384]{1,0:T(8,128)S(1)}, u32[]{:S(2)}, u32[]{:S(2)}) collective-permute-start(f32[256,384]{1,0:T(8,128)S(1)} %get-tuple-element.76), channel_id=1, source_target_pairs={{0,1},{8,9},{2,3},{10,11},{4,5},{12,13},{6,7},{14,15},{1,0},{9,8},... | collective-permute-start | bytes 1179656 | tf_op jit(solution)/shard_map/ppermute | solution.py:25
  63.3 6.2 %collective-permute-start.13 = (f32[48,384]{1,0:T(8,128)S(1)}, f32[48,384]{1,0:T(8,128)S(1)}, u32[]{:S(2)}, u32[]{:S(2)}) collective-permute-start(f32[48,384]{1,0:T(8,128)S(1)} %get-tuple-element.86), channel_id=1, source_target_pairs={{0,4},{8,12},{2,6},{10,14},{4,0},{12,8},{6,2},{14,10},{1,5},{9,13}... | collective-permute-start | bytes 221192 | tf_op jit(solution)/shard_map/ppermute | solution.py:21
  65.4 4.9 %collective-permute-start.14 = (f32[48,384]{1,0:T(8,128)S(1)}, f32[48,384]{1,0:T(8,128)S(1)}, u32[]{:S(2)}, u32[]{:S(2)}) collective-permute-start(f32[48,384]{1,0:T(8,128)S(1)} %get-tuple-element.88), channel_id=1, source_target_pairs={{0,2},{8,10},{2,4},{10,12},{4,6},{12,14},{6,0},{14,8},{1,3},{9,11}... | collective-permute-start | bytes 221192 | tf_op jit(solution)/shard_map/ppermute | solution.py:21
  65.4 5.3 %collective-permute-start.15 = (f32[48,384]{1,0:T(8,128)S(1)}, f32[48,384]{1,0:T(8,128)S(1)}, u32[]{:S(2)}, u32[]{:S(2)}) collective-permute-start(f32[48,384]{1,0:T(8,128)S(1)} %get-tuple-element.87), channel_id=1, source_target_pairs={{0,6},{8,14},{2,0},{10,8},{4,2},{12,10},{6,4},{14,12},{1,7},{9,15}... | collective-permute-start | bytes 221192 | tf_op jit(solution)/shard_map/ppermute | solution.py:21
  70.8 8.4 %collective-permute-start.16 = (f32[48,384]{1,0:T(8,128)S(1)}, f32[48,384]{1,0:T(8,128)S(1)}, u32[]{:S(2)}, u32[]{:S(2)}) collective-permute-start(f32[48,384]{1,0:T(8,128)S(1)} %add_add_fusion.1), channel_id=1, source_target_pairs={{0,16},{8,24},{2,18},{10,26},{4,20},{12,28},{6,22},{14,30},{1,17},... | collective-permute-start | bytes 221192 | tf_op jit(solution)/shard_map/ppermute | solution.py:21
  73.1 6.1 %collective-permute-start.17 = (f32[48,384]{1,0:T(8,128)S(1)}, f32[48,384]{1,0:T(8,128)S(1)}, u32[]{:S(2)}, u32[]{:S(2)}) collective-permute-start(f32[48,384]{1,0:T(8,128)S(1)} %add_add_fusion.1), channel_id=1, source_target_pairs={{0,1},{8,9},{2,3},{10,11},{4,5},{12,13},{6,7},{14,15},{1,16},{9,24... | collective-permute-start | bytes 221192 | tf_op jit(solution)/shard_map/ppermute | solution.py:21
  74.0 5.3 %collective-permute-start.18 = (f32[48,384]{1,0:T(8,128)S(1)}, f32[48,384]{1,0:T(8,128)S(1)}, u32[]{:S(2)}, u32[]{:S(2)}) collective-permute-start(f32[48,384]{1,0:T(8,128)S(1)} %add_add_fusion.1), channel_id=1, source_target_pairs={{0,17},{8,25},{2,19},{10,27},{4,21},{12,29},{6,23},{14,31},{1,0},{... | collective-permute-start | bytes 221192 | tf_op jit(solution)/shard_map/ppermute | solution.py:21
  77.2 6.9 %collective-permute-start.19 = (f32[128,384]{1,0:T(8,128)S(1)}, f32[128,384]{1,0:T(8,128)S(1)}, u32[]{:S(2)}, u32[]{:S(2)}) collective-permute-start(f32[128,384]{1,0:T(8,128)S(1)} %constant_dynamic-slice_fusion.6), channel_id=1, source_target_pairs={{0,32},{32,0},{64,96},{96,64},{128,160},{160,128},{192,224},{224,1... | collective-permute-start | bytes 589832 | tf_op jit(solution)/shard_map/ppermute | solution.py:33
  79.2 4.8 %collective-permute-start.20 = (f32[48,384]{1,0:T(8,128)S(1)}, f32[48,384]{1,0:T(8,128)S(1)}, u32[]{:S(2)}, u32[]{:S(2)}) collective-permute-start(f32[48,384]{1,0:T(8,128)S(1)} %get-tuple-element.84), channel_id=1, source_target_pairs={{0,32},{32,0},{64,96},{96,64},{128,160},{160,128},{192,224},{224,1... | collective-permute-start | bytes 221192 | tf_op jit(solution)/shard_map/ppermute | solution.py:33
  84.2 12.2 %collective-permute-start.21 = (f32[80,384]{1,0:T(8,128)S(1)}, f32[80,384]{1,0:T(8,128)S(1)}, u32[]{:S(2)}, u32[]{:S(2)}) collective-permute-start(f32[80,384]{1,0:T(8,128)S(1)} %get-tuple-element.94), channel_id=1, source_target_pairs={{0,128},{32,160},{64,192},{96,224},{128,0},{160,32},{192,64},{224,... | collective-permute-start | bytes 368648 | tf_op jit(solution)/shard_map/ppermute | solution.py:29
  91.7 8.7 %collective-permute-start.22 = (f32[80,384]{1,0:T(8,128)S(1)}, f32[80,384]{1,0:T(8,128)S(1)}, u32[]{:S(2)}, u32[]{:S(2)}) collective-permute-start(f32[80,384]{1,0:T(8,128)S(1)} %get-tuple-element.95), channel_id=1, source_target_pairs={{0,64},{32,96},{64,128},{96,160},{128,192},{160,224},{192,0},{224,... | collective-permute-start | bytes 368648 | tf_op jit(solution)/shard_map/ppermute | solution.py:29
  92.8 8.4 %collective-permute-start.23 = (f32[80,384]{1,0:T(8,128)S(1)}, f32[80,384]{1,0:T(8,128)S(1)}, u32[]{:S(2)}, u32[]{:S(2)}) collective-permute-start(f32[80,384]{1,0:T(8,128)S(1)} %get-tuple-element.93), channel_id=1, source_target_pairs={{0,192},{32,224},{64,0},{96,32},{128,64},{160,96},{192,128},{224,1... | collective-permute-start | bytes 368648 | tf_op jit(solution)/shard_map/ppermute | solution.py:29
  101.2 7.1 %collective-permute-start.28 = (f32[32,384]{1,0:T(8,128)S(1)}, f32[32,384]{1,0:T(8,128)S(1)}, u32[]{:S(2)}, u32[]{:S(2)}) collective-permute-start(f32[32,384]{1,0:T(8,128)S(1)} %slice.23), channel_id=1, source_target_pairs={{0,32},{32,0},{64,96},{96,64},{128,160},{160,128},{192,224},{224,1... | collective-permute-start | bytes 147464 | tf_op jit(solution)/shard_map/ppermute | solution.py:33
  102.2 11.7 %collective-permute-start.24 = (f32[2,48,384]{2,1,0:T(8,128)S(1)}, f32[2,48,384]{2,1,0:T(8,128)S(1)}, u32[]{:S(2)}, u32[]{:S(2)}) collective-permute-start(f32[2,48,384]{2,1,0:T(8,128)S(1)} %pad_maximum_fusion.4), channel_id=1, source_target_pairs={{0,6},{8,14},{2,0},{10,8},{4,2},{12,10},{6,4},{14,12},{1,7},{9,15}... | collective-permute-start | bytes 442376 | tf_op jit(solution)/shard_map/ppermute | solution.py:21
  103.7 11.8 %collective-permute-start.25 = (f32[2,48,384]{2,1,0:T(8,128)S(1)}, f32[2,48,384]{2,1,0:T(8,128)S(1)}, u32[]{:S(2)}, u32[]{:S(2)}) collective-permute-start(f32[2,48,384]{2,1,0:T(8,128)S(1)} %pad_maximum_fusion.4), channel_id=1, source_target_pairs={{0,4},{8,12},{2,6},{10,14},{4,0},{12,8},{6,2},{14,10},{1,5},{9,13}... | collective-permute-start | bytes 442376 | tf_op jit(solution)/shard_map/ppermute | solution.py:21
  105.8 9.6 %collective-permute-start.26 = (f32[2,48,384]{2,1,0:T(8,128)S(1)}, f32[2,48,384]{2,1,0:T(8,128)S(1)}, u32[]{:S(2)}, u32[]{:S(2)}) collective-permute-start(f32[2,48,384]{2,1,0:T(8,128)S(1)} %pad_maximum_fusion.4), channel_id=1, source_target_pairs={{0,2},{8,10},{2,4},{10,12},{4,6},{12,14},{6,0},{14,8},{1,3},{9,11}... | collective-permute-start | bytes 442376 | tf_op jit(solution)/shard_map/ppermute | solution.py:21
  108.3 10.8 %collective-permute-start.29 = (f32[64,384]{1,0:T(8,128)S(1)}, f32[64,384]{1,0:T(8,128)S(1)}, u32[]{:S(2)}, u32[]{:S(2)}) collective-permute-start(f32[64,384]{1,0:T(8,128)S(1)} %fusion.3), channel_id=1, source_target_pairs={{0,192},{32,224},{64,0},{96,32},{128,64},{160,96},{192,128},{224,1... | collective-permute-start | bytes 294920 | tf_op jit(solution)/shard_map/ppermute | solution.py:29
  112.2 9.8 %collective-permute-start.30 = (f32[64,384]{1,0:T(8,128)S(1)}, f32[64,384]{1,0:T(8,128)S(1)}, u32[]{:S(2)}, u32[]{:S(2)}) collective-permute-start(f32[64,384]{1,0:T(8,128)S(1)} %fusion.3), channel_id=1, source_target_pairs={{0,128},{32,160},{64,192},{96,224},{128,0},{160,32},{192,64},{224,... | collective-permute-start | bytes 294920 | tf_op jit(solution)/shard_map/ppermute | solution.py:29
  113.9 8.1 %collective-permute-start.31 = (f32[64,384]{1,0:T(8,128)S(1)}, f32[64,384]{1,0:T(8,128)S(1)}, u32[]{:S(2)}, u32[]{:S(2)}) collective-permute-start(f32[64,384]{1,0:T(8,128)S(1)} %fusion.3), channel_id=1, source_target_pairs={{0,64},{32,96},{64,128},{96,160},{128,192},{160,224},{192,0},{224,... | collective-permute-start | bytes 294920 | tf_op jit(solution)/shard_map/ppermute | solution.py:29
  115.6 7.3 %collective-permute-start.27 = (f32[2,192,384]{2,1,0:T(8,128)S(1)}, f32[2,192,384]{2,1,0:T(8,128)S(1)}, u32[]{:S(2)}, u32[]{:S(2)}) collective-permute-start(f32[2,192,384]{2,1,0:T(8,128)S(1)} %constant_dynamic-slice_fusion.1.mine), channel_id=1, source_target_pairs={{0,8},{8,0},{2,10},{10,2},{4,12},{12,4},{6,14},{14,6},{1,9},{9,1},... | collective-permute-start | bytes 1769480 | tf_op jit(solution)/shard_map/ppermute | solution.py:21
